TPU v7x, 32 devices: a whole 2x2x4 slice. The times are simulated.
32 devices in a mesh: frames: 4 (over z), mp: 4 (over x, core), dp: 2 (over y).
Axes of the slice: x: 2, y: 2, z: 4, core: 2. Of those that a mesh axis runs over, the one named last changes fastest.
Arguments:
- projections: bfloat16 [2, 8, 96, 3, 3584], P('dp', 'frames', None, None, 'mp'), may hold values from -18 to 18
- perturbation: bfloat16 [2, 8, 96, 3, 3584], P('dp', 'frames', None, None, 'mp'), may hold values from -44 to 44
- out_weight: bfloat16 [3584, 3584], P('frames', 'mp'), may hold values from -0.09375 to 0.09375
- norm_gain: float32 [3584], P('mp'), may hold values from 0.25 to 1.75
- live_counts: int32 [2, 8], P('dp'), may hold values from 72 to 96, as said below
Outputs:
- features: bfloat16 [2, 8, 96, 3584], P('dp', 'frames', None, 'mp')
- penalty: float32 [2], P('dp')
- gain_grad: float32 [3584], P('mp')
Inputs may be any that keep to these rules, and one draw needn't show every extreme that they name: `live_counts`: in each clip one slot has all 96 tokens live and another has 72 live.
All inputs are finite; a program needn't handle non-finite values.
Results may differ from a plain program's by a relative error of at most 0.0057.
Values may be sent and summed in bfloat16 or wider, within the bound.
No kernel may reach another device: no remote copies, remote signals or barrier semaphores. Data moves between devices by JAX's collectives and lax.ppermute only.
A program may use at most 64 MiB of HBM per device.

v0:
```python
import math

import jax
import jax.numpy as jnp
from jax import lax
from jax.experimental import pallas as pl
from jax.experimental.pallas import tpu as pltpu
from jax.sharding import PartitionSpec as P

HEAD_DIM = 128
HEADS_AT_ONCE = 1


sigma_noise = 0.25
epsilon = 1e-06


def perturb(clean, noise):
    return (clean.astype(jnp.float32) + sigma_noise * noise.astype(jnp.float32)).astype(jnp.bfloat16)


def attend_kernel(counts_ref, own_ref, left_ref, right_ref, out_ref):
    slots, _, tile_len, width = own_ref.shape
    key_pos = lax.broadcasted_iota(jnp.int32, (1, 2 * tile_len), 1)
    live = []
    for slot in range(slots):
        own_count = counts_ref[slot + 1]
        far_count = counts_ref[0 if slot == 0 else slots + 1]
        live.append((key_pos < own_count) | ((key_pos >= tile_len) & (key_pos < tile_len + far_count)))
    units = [(slot, head) for head in range(width // HEAD_DIM) for slot in range(slots)]

    scores = []
    for slot, head in units:
        cols = pl.ds(head * HEAD_DIM, HEAD_DIM)
        halo_ref = left_ref if slot == 0 else right_ref
        keys = jnp.concatenate([own_ref[slot, 1, :, cols], halo_ref[0, :, cols]], axis=0)
        raw = lax.dot_general(
            own_ref[slot, 0, :, cols],
            keys,
            (((1,), (1,)), ((), ())),
            preferred_element_type=jnp.float32,
        )
        scores.append(jnp.where(live[slot], raw * (1.0 / math.sqrt(HEAD_DIM)), jnp.float32(-1e30)))
    largest = [jnp.max(s, axis=-1, keepdims=True) for s in scores]
    weights = [jnp.exp(s - top) for s, top in zip(scores, largest)]
    totals = [jnp.sum(w, axis=-1, keepdims=True) for w in weights]
    for (slot, head), weight, total in zip(units, weights, totals):
        cols = pl.ds(head * HEAD_DIM, HEAD_DIM)
        halo_ref = left_ref if slot == 0 else right_ref
        values = jnp.concatenate([own_ref[slot, 2, :, cols], halo_ref[1, :, cols]], axis=0)
        probabilities = (weight * (1.0 / total)).astype(jnp.bfloat16)
        out_ref[slot, :, cols] = jnp.dot(
            probabilities, values, preferred_element_type=jnp.float32
        ).astype(jnp.bfloat16)


def attention(nearby, own, left, right):
    slots, _, tile_len, width = own.shape
    block = HEADS_AT_ONCE * HEAD_DIM
    own_spec = pl.BlockSpec((slots, 3, tile_len, block), lambda h, c: (0, 0, 0, h))
    halo_spec = pl.BlockSpec((2, tile_len, block), lambda h, c: (0, 0, h))
    return pl.pallas_call(
        attend_kernel,
        grid_spec=pltpu.PrefetchScalarGridSpec(
            num_scalar_prefetch=1,
            grid=(width // block,),
            in_specs=[own_spec, halo_spec, halo_spec],
            out_specs=pl.BlockSpec((slots, tile_len, block), lambda h, c: (0, 0, h)),
        ),
        out_shape=jax.ShapeDtypeStruct((slots, tile_len, width), jnp.bfloat16),
        compiler_params=pltpu.CompilerParams(vmem_limit_bytes=24 * 1024 * 1024),
        cost_estimate=pl.CostEstimate(
            flops=16 * slots * tile_len * tile_len * width,
            bytes_accessed=12 * slots * tile_len * width,
            transcendentals=0,
        ),
        name="attention",
    )(nearby, own, left, right)


def project_kernel(shard_total, with_total, places_ref, *refs):
    rows_ref = refs[0]
    weight_refs = refs[1 : 1 + shard_total]
    out_ref = refs[-1]
    shard = pl.program_id(1)

    def add(weight_ref, first):
        term = jnp.dot(
            rows_ref[0, 0], weight_ref[...], preferred_element_type=jnp.float32
        )
        if not first:
            out_ref[0] = out_ref[0] + term
        elif with_total:
            out_ref[0] = refs[1 + shard_total][0] + term
        else:
            out_ref[0] = term

    for n in range(shard_total):
        pl.when(shard == n)(lambda n=n: add(weight_refs[n], n == 0))


def project(places, clip_index, rows, weights, total):
    _, clip_count, row_count, depth = rows.shape
    columns = weights[0].shape[1]
    shard_total = len(weights)
    scalars = jnp.concatenate([jnp.stack(places), clip_index[None]]).astype(jnp.int32)
    out_spec = pl.BlockSpec((1, row_count, columns), lambda c, j, s: (c, 0, 0))
    operands = [rows, *weights]
    in_specs = [
        pl.BlockSpec(
            (1, 1, row_count, depth), lambda c, j, s: (s[j], c ^ s[shard_total], 0, 0)
        )
    ] + [pl.BlockSpec((depth, columns), lambda c, j, s: (0, 0)) for _ in weights]
    if total is not None:
        operands.append(total)
        in_specs.append(out_spec)

    def kernel(*refs):
        project_kernel(shard_total, total is not None, *refs)

    return pl.pallas_call(
        kernel,
        grid_spec=pltpu.PrefetchScalarGridSpec(
            num_scalar_prefetch=1,
            grid=(clip_count, shard_total),
            in_specs=in_specs,
            out_specs=out_spec,
        ),
        out_shape=jax.ShapeDtypeStruct((clip_count, row_count, columns), jnp.float32),
        compiler_params=pltpu.CompilerParams(vmem_limit_bytes=40 * 1024 * 1024),
        cost_estimate=pl.CostEstimate(
            flops=2 * clip_count * row_count * depth * columns * shard_total,
            bytes_accessed=shard_total * depth * (clip_count * row_count + columns) * 2,
            transcendentals=0,
        ),
        name="project",
    )(scalars, *operands)


def swap(array, axis, distance):
    count = lax.axis_size(axis)
    return lax.ppermute(array, axis, [(i, i ^ distance) for i in range(count)])


def distances(axis):
    count = lax.axis_size(axis)
    return [(axis, 1 << bit) for bit in reversed(range(count.bit_length() - 1))]


def spread(block, order):
    blocks = {(0, 0): block}
    for axis, distance in order:
        for (model, clip), held in list(blocks.items()):
            key = (model ^ distance, clip) if axis == "mp" else (model, clip ^ distance)
            blocks[key] = swap(held, axis, distance)
    return blocks


def add_up(array, order):
    for axis, distance in order:
        array = array + swap(array, axis, distance)
    return array


def pick(options, index):
    return lax.select_n(index, *options) if len(options) > 1 else options[0]


def local(projections, perturbation, out_weight, norm_gain, live_counts):
    tile_len = projections.shape[2]
    local_width = projections.shape[4]
    slots = projections.shape[1]
    slab_count = lax.axis_size("frames")
    slab_index = lax.axis_index("frames")
    model_count = lax.axis_size("mp")
    model_index = lax.axis_index("mp")
    clip_count = lax.axis_size("dp")
    clip_index = lax.axis_index("dp")
    model_width = local_width * model_count
    token_total = slots * slab_count * tile_len
    half = local_width // clip_count
    near_rows = slots * tile_len

    def own_columns(array):
        return pick(
            [array[..., n * half : (n + 1) * half] for n in range(clip_count)], clip_index
        )

    clean = projections[0].transpose(0, 2, 1, 3)
    noise = perturbation[0].transpose(0, 2, 1, 3)
    perturbed = perturb(clean, noise)
    up = [(i, i + 1) for i in range(slab_count - 1)]
    down = [(i + 1, i) for i in range(slab_count - 1)]

    own_weight = own_columns(out_weight)
    shards = [(own_weight, slab_index)]
    line = slab_count == model_count
    if line:
        rising = falling = own_weight
        for step in range(1, slab_count):
            rising = lax.ppermute(rising, "frames", up[step - 1 :])
            falling = lax.ppermute(falling, "frames", down[: slab_count - step])
            shards += [
                (rising, jnp.maximum(slab_index - step, 0)),
                (falling, jnp.minimum(slab_index + step, slab_count - 1)),
            ]

    spread_counts = spread(live_counts[0], distances("dp"))
    counts = [
        pick([spread_counts[0, c ^ d] for d in range(clip_count)], clip_index)
        for c in range(clip_count)
    ]
    near_counts = [
        lax.dynamic_slice_in_dim(jnp.pad(n, (1, 1)), slots * slab_index, slots + 2) for n in counts
    ]
    nearby = pick(near_counts, clip_index)

    gathered = []
    for stream, order in (
        (clean, distances("dp") + distances("mp")),
        (perturbed, distances("mp")[:1] + distances("dp") + distances("mp")[1:]),
    ):
        left = lax.ppermute(stream[slots - 1, 1:], "frames", up)
        right = lax.ppermute(stream[0, 1:], "frames", down)
        attended = attention(nearby, stream, left, right)
        gathered.append(spread(attended.reshape(near_rows, local_width), order))
    rows = jnp.stack(
        [
            jnp.stack(
                [jnp.concatenate([g[m, c] for g in gathered], axis=0) for c in range(clip_count)]
            )
            for m in range(model_count)
        ]
    )

    if line:
        early, late = shards[:-2], shards[-2:]
        total = project(
            [place ^ model_index for _, place in early],
            clip_index,
            rows,
            [weight for weight, _ in early],
            None,
        )
        total = project(
            [place ^ model_index for _, place in late],
            clip_index,
            rows,
            [weight for weight, _ in late],
            total,
        )
    else:
        weight = lax.all_gather(own_weight, "frames", axis=0, tiled=True)
        weight = weight.reshape(model_count, local_width, half)
        total = project(
            [jnp.int32(m) for m in range(model_count)],
            clip_index,
            rows,
            [
                lax.dynamic_index_in_dim(weight, model_index ^ m, 0, keepdims=False)
                for m in range(model_count)
            ],
            None,
        )
    projected = total.reshape(clip_count, 2, slots, tile_len, half)

    everyone = distances("dp") + distances("mp")
    squares = add_up(jnp.sum(projected * projected, axis=-1), everyone)
    scale = lax.rsqrt(squares / model_width + epsilon)[..., None]
    own_counts = jnp.stack([n[1 : slots + 1] for n in near_counts])
    live = (jnp.arange(tile_len) < own_counts[..., None]).astype(jnp.float32)[..., None]
    gain = own_columns(norm_gain)
    normed = projected * scale
    features = (normed[:, 0] * gain * live).astype(jnp.bfloat16)
    difference = (normed[:, 1] - normed[:, 0]) * live
    feature_sums = jnp.sum(difference * difference, axis=(1, 2))
    penalties = jnp.sum(feature_sums * gain * gain, axis=-1)

    columns = [pick([features[d] for d in range(clip_count)], clip_index)]
    for distance in range(1, clip_count):
        sent = pick([features[d ^ distance] for d in range(clip_count)], clip_index)
        columns.append(swap(sent, "dp", distance))
    features = jnp.concatenate(
        [
            pick([columns[n ^ d] for d in range(clip_count)], clip_index)
            for n in range(clip_count)
        ],
        axis=-1,
    )[None]

    sums = jnp.concatenate([jnp.sum(feature_sums, axis=0), penalties])
    sums = add_up(sums, distances("frames"))
    gain_halves = spread(sums[:half] * gain, distances("dp"))
    gain_grad = jnp.concatenate(
        [
            pick([gain_halves[0, n ^ d] for d in range(clip_count)], clip_index)
            for n in range(clip_count)
        ]
    ) / (sigma_noise * sigma_noise * token_total)
    penalties = add_up(sums[half:], everyone)
    penalty = pick([penalties[d : d + 1] for d in range(clip_count)], clip_index) / (
        sigma_noise * sigma_noise * token_total * model_width
    )
    return (features, penalty, gain_grad)


def solution(mesh):
    placed = (
        P("dp", "frames", None, None, "mp"),
        P("dp", "frames", None, None, "mp"),
        P("frames", "mp"),
        P("mp"),
        P("dp", None),
    )
    return jax.shard_map(
        local,
        mesh=mesh,
        in_specs=placed,
        out_specs=(P("dp", "frames", None, "mp"), P("dp"), P("mp")),
        check_vma=False,
    )
```

profile of v0, /device:TPU:0, one launch (start us, length us, event | category | flops | bytes accessed | tf_op | source)
XLA Modules:
  0.0 164.3 jit_solution(5129012343598642673)
XLA Ops:
  0.6 3.0 %collective-permute-start = (s32[8]{0:T(128)}, s32[8]{0:T(128)S(1)}, u32[]{:S(2)}, u32[]{:S(2)}) collective-permute-start(s32[8]{0:T(128)} %bitcast.101), channel_id=1, source_target_pairs={{0,1},{1,0},{2,3},{3,2},{4,5},{5,4},{6,7},{7,6},{8,9},{9,8},{10,11... | collective-permute-start | bytes 104 | tf_op jit(solution)/shard_map/ppermute | solution.py:142
  5.7 3.5 %collective-permute-start.1 = (bf16[2,96,896]{2,1,0:T(8,128)(2,1)}, bf16[2,96,896]{2,1,0:T(8,128)(2,1)S(1)}, u32[]{:S(2)}, u32[]{:S(2)}) collective-permute-start(bf16[2,96,896]{2,1,0:T(8,128)(2,1)} %get-tuple-element.10), channel_id=1, source_target_pairs={{0,8},{8,16},{16,24},{1,9},{9,17},{17,25},{2,10},{10,18},{18,26},{... | collective-permute-start | bytes 1032200 | tf_op jit(solution)/shard_map/ppermute | solution.py:223
  12.9 4.6 %collective-permute-start.3 = (bf16[2,96,896]{2,1,0:T(8,128)(2,1)}, bf16[2,96,896]{2,1,0:T(8,128)(2,1)S(1)}, u32[]{:S(2)}, u32[]{:S(2)}) collective-permute-start(bf16[2,96,896]{2,1,0:T(8,128)(2,1)} %get-tuple-element.12), channel_id=1, source_target_pairs={{0,8},{8,16},{16,24},{1,9},{9,17},{17,25},{2,10},{10,18},{18,26},{... | collective-permute-start | bytes 1032200 | tf_op jit(solution)/shard_map/ppermute | solution.py:223
  22.3 4.5 %attention.2 = bf16[2,96,896]{2,1,0:T(8,128)(2,1)S(1)} custom-call(s32[4]{0:T(128)S(1)} %get-tuple-element.5.counts_ref, bf16[2,3,96,896]{3,2,1,0:T(8,128)(2,1)S(1)} %bitcast.92, bf16[2,96,896]{2,1,0:T(8,128)(2,1)S(1)} %collective-permute-done.1.left_ref, bf16[2,96,896]{2,1,0:T(8,128)(2,1)S(1)} %copy-done.10), custom_call_target="tpu_custom_call" | custom-call | flops 264241152 | bytes 2064384 | tf_op jit(solution)/shard_map/attention/pallas_call | solution.py:62
  28.3 4.5 %attention.3 = bf16[2,96,896]{2,1,0:T(8,128)(2,1)S(1)} custom-call(s32[4]{0:T(128)S(1)} %get-tuple-element.5.counts_ref, bf16[2,3,96,896]{3,2,1,0:T(8,128)(2,1)S(1)} %fusion.own_ref, bf16[2,96,896]{2,1,0:T(8,128)(2,1)S(1)} %collective-permute-done.3.left_ref, bf16[2,96,896]{2,1,0:T(8,128)(2,1)S(1)} %collective-permute-done.4.right_ref), custom_call_target="tpu_custom_call" | custom-call | flops 264241152 | bytes 2064384 | tf_op jit(solution)/shard_map/attention/pallas_call | solution.py:62
  35.1 4.4 %collective-permute-start.19 = (bf16[896,448]{0,1:T(8,128)(2,1)}, bf16[896,448]{0,1:T(8,128)(2,1)}, u32[]{:S(2)}, u32[]{:S(2)}) collective-permute-start(bf16[896,448]{0,1:T(8,128)(2,1)} %copy.21), channel_id=1, source_target_pairs={{0,8},{8,16},{16,24},{1,9},{9,17},{17,25},{2,10},{10,18},{18,26},{... | collective-permute-start | bytes 2408456 | tf_op jit(solution)/shard_map/ppermute | solution.py:201
  45.9 7.7 %collective-permute-done.12 = bf16[192,896]{1,0:T(8,128)(2,1)} collective-permute-done((bf16[192,896]{1,0:T(8,128)(2,1)S(1)}, bf16[192,896]{1,0:T(8,128)(2,1)}, u32[]{:S(2)}, u32[]{:S(2)}) %collective-permute-start.12) | collective-permute-done | bytes 344096 | tf_op jit(solution)/shard_map/ppermute | solution.py:142
  55.1 5.9 %collective-permute-done.11 = bf16[192,896]{1,0:T(8,128)(2,1)} collective-permute-done((bf16[192,896]{1,0:T(8,128)(2,1)S(1)}, bf16[192,896]{1,0:T(8,128)(2,1)}, u32[]{:S(2)}, u32[]{:S(2)}) %collective-permute-start.11) | collective-permute-done | bytes 344096 | tf_op jit(solution)/shard_map/ppermute | solution.py:142
  64.6 2.2 %copy.23.refs_3_ = bf16[896,448]{1,0:T(8,128)(2,1)} copy(bf16[896,448]{0,1:T(8,128)(2,1)} %collective-permute-done.19) | data formatting | bytes 1605632 | tf_op jit(solution)/shard_map/ppermute | solution.py:201
  66.8 2.3 %copy.24.refs_4_ = bf16[896,448]{1,0:T(8,128)(2,1)} copy(bf16[896,448]{0,1:T(8,128)(2,1)} %collective-permute-done.22) | data formatting | bytes 1605632 | tf_op jit(solution)/shard_map/ppermute | solution.py:202
  78.3 17.1 %collective-permute-done.23 = bf16[896,448]{0,1:T(8,128)(2,1)} collective-permute-done((bf16[896,448]{0,1:T(8,128)(2,1)}, bf16[896,448]{0,1:T(8,128)(2,1)}, u32[]{:S(2)}, u32[]{:S(2)}) %collective-permute-start.23) | collective-permute-done | bytes 802848 | tf_op jit(solution)/shard_map/ppermute | solution.py:202
  96.9 3.1 %pad_maximum_fusion.refs_1_ = bf16[4,2,384,896]{3,2,1,0:T(8,128)(2,1)} fusion(bf16[1,2,384,896]{3,2,1,0:T(8,128)(2,1)S(1)} %maximum_bitcast_fusion.3, bf16[1,2,384,896]{3,2,1,0:T(8,128)(2,1)S(1)} %maximum_bitcast_fusion.2, bf16[1,2,384,896]{3,2,1,0:T(8,128)(2,1)S(1)} %maximum_bitcast_fusion.1, bf16[1,2,384,896]{3,2,1,0:T(8,128)(2,1)S(1)} %maximum_bitcast_fusion), kind=kLoop, calls=%fused_computation | loop fusion | flops 8257536 | bytes 11010048 | tf_op jit(solution)/shard_map/stack | solution.py:227
  99.9 2.3 %copy.25.refs_5_ = bf16[896,448]{1,0:T(8,128)(2,1)} copy(bf16[896,448]{0,1:T(8,128)(2,1)} %collective-permute-done.20) | data formatting | bytes 1605632 | tf_op jit(solution)/shard_map/ppermute | solution.py:201
  102.2 2.2 %copy.26.refs_6_ = bf16[896,448]{1,0:T(8,128)(2,1)} copy(bf16[896,448]{0,1:T(8,128)(2,1)} %collective-permute-done.23) | data formatting | bytes 1605632 | tf_op jit(solution)/shard_map/ppermute | solution.py:202
  104.4 2.6 %copy-done = bf16[4,2,384,896]{3,2,1,0:T(8,128)(2,1)S(1)} copy-done((bf16[4,2,384,896]{3,2,1,0:T(8,128)(2,1)S(1)}, bf16[4,2,384,896]{3,2,1,0:T(8,128)(2,1)}, u32[]{:S(2)}) %copy-start) | copy-done | bytes 5505048
  111.7 6.6 %project.2.refs_4_ = f32[2,384,448]{2,1,0:T(8,128)S(1)} custom-call(s32[6]{0:T(128)S(1)} %concatenate.48.refs_0_, bf16[4,2,384,896]{3,2,1,0:T(8,128)(2,1)S(1)} %copy-done, bf16[896,448]{1,0:T(8,128)(2,1)S(1)} %slice_select_fusion.refs_2_, bf16[896,448]{1,0:T(8,128)(2,1)S(1)} %copy-done.3, bf16[896,448]{1,0:T(8,128)(2,1)S(1)} %copy-done.4, ...), custom_call_target="tpu_custom_call" | custom-call | flops 3082813440 | bytes 10895360 | tf_op jit(solution)/shard_map/project/pallas_call | solution.py:121
  118.3 2.3 %copy.27.refs_2_ = bf16[896,448]{1,0:T(8,128)(2,1)} copy(bf16[896,448]{0,1:T(8,128)(2,1)} %collective-permute-done.21) | data formatting | bytes 1605632 | tf_op jit(solution)/shard_map/ppermute | solution.py:201
  120.5 2.3 %copy.28.refs_3_ = bf16[896,448]{1,0:T(8,128)(2,1)} copy(bf16[896,448]{0,1:T(8,128)(2,1)} %collective-permute-done.24) | data formatting | bytes 1605632 | tf_op jit(solution)/shard_map/ppermute | solution.py:202
  122.8 2.6 %copy-done.1 = bf16[4,2,384,896]{3,2,1,0:T(8,128)(2,1)S(1)} copy-done((bf16[4,2,384,896]{3,2,1,0:T(8,128)(2,1)S(1)}, bf16[4,2,384,896]{3,2,1,0:T(8,128)(2,1)}, u32[]{:S(2)}) %copy-start.1) | copy-done | bytes 5505048
  127.7 2.9 %project.3 = f32[2,384,448]{2,1,0:T(8,128)S(1)} custom-call(s32[3]{0:T(128)S(1)} %pad_add_fusion.1.refs_0_, bf16[4,2,384,896]{3,2,1,0:T(8,128)(2,1)S(1)} %copy-done.1, bf16[896,448]{1,0:T(8,128)(2,1)S(1)} %copy-done.7, bf16[896,448]{1,0:T(8,128)(2,1)S(1)} %copy-done.8, f32[2,384,448]{2,1,0:T(8,128)S(1)} %project.2.refs_4_), custom_call_target="tpu_custom_call" | custom-call | flops 1233125376 | bytes 4358144 | tf_op jit(solution)/shard_map/project/pallas_call | solution.py:121
  136.1 2.1 %collective-permute-done.26 = f32[2,2,2,96]{3,2,1,0:T(2,128)S(1)} collective-permute-done((f32[2,2,2,96]{3,2,1,0:T(2,128)S(1)}, f32[2,2,2,96]{3,2,1,0:T(2,128)S(1)}, u32[]{:S(2)}, u32[]{:S(2)}) %collective-permute-start.26) | collective-permute-done | bytes 3104 | tf_op jit(solution)/shard_map/ppermute | solution.py:142
  140.0 2.9 %collective-permute-start.29 = (f32[450]{0:T(512)S(1)}, f32[450]{0:T(512)S(1)}, u32[]{:S(2)}, u32[]{:S(2)}) collective-permute-start(f32[450]{0:T(512)S(1)} %pad_maximum_fusion.1), channel_id=1, source_target_pairs={{0,16},{8,24},{16,0},{24,8},{1,17},{9,25},{17,1},{25,9},{2,18},{10... | collective-permute-start | bytes 5408 | tf_op jit(solution)/shard_map/ppermute | solution.py:142
  144.6 3.5 %collective-permute-start.30 = (f32[450]{0:T(512)S(1)}, f32[450]{0:T(512)S(1)}, u32[]{:S(2)}, u32[]{:S(2)}) collective-permute-start(f32[450]{0:T(512)S(1)} %fusion.7), channel_id=1, source_target_pairs={{0,8},{8,0},{16,24},{24,16},{1,9},{9,1},{17,25},{25,17},{2,10},{10... | collective-permute-start | bytes 5408 | tf_op jit(solution)/shard_map/ppermute | solution.py:142
  151.9 3.0 %collective-permute-done.31 = f32[2]{0:T(128)S(1)} collective-permute-done((f32[2]{0:T(128)S(1)}, f32[2]{0:T(128)S(1)}, u32[]{:S(2)}, u32[]{:S(2)}) %collective-permute-start.31) | collective-permute-done | bytes 40 | tf_op jit(solution)/shard_map/ppermute | solution.py:142
  (141 shorter events, 62.9 us)
Async XLA Ops:
  0.6 18.2 %collective-permute-start = (s32[8]{0:T(128)}, s32[8]{0:T(128)S(1)}, u32[]{:S(2)}, u32[]{:S(2)}) collective-permute-start(s32[8]{0:T(128)} %bitcast.101), channel_id=1, source_target_pairs={{0,1},{1,0},{2,3},{3,2},{4,5},{5,4},{6,7},{7,6},{8,9},{9,8},{10,11... | collective-permute-start | bytes 104 | tf_op jit(solution)/shard_map/ppermute | solution.py:142
  5.7 13.2 %collective-permute-start.1 = (bf16[2,96,896]{2,1,0:T(8,128)(2,1)}, bf16[2,96,896]{2,1,0:T(8,128)(2,1)S(1)}, u32[]{:S(2)}, u32[]{:S(2)}) collective-permute-start(bf16[2,96,896]{2,1,0:T(8,128)(2,1)} %get-tuple-element.10), channel_id=1, source_target_pairs={{0,8},{8,16},{16,24},{1,9},{9,17},{17,25},{2,10},{10,18},{18,26},{... | collective-permute-start | bytes 1032200 | tf_op jit(solution)/shard_map/ppermute | solution.py:223
  9.2 11.3 %collective-permute-start.2 = (bf16[2,96,896]{2,1,0:T(8,128)(2,1)}, bf16[2,96,896]{2,1,0:T(8,128)(2,1)S(1)}, u32[]{:S(2)}, u32[]{:S(2)}) collective-permute-start(bf16[2,96,896]{2,1,0:T(8,128)(2,1)} %get-tuple-element.9), channel_id=1, source_target_pairs={{8,0},{16,8},{24,16},{9,1},{17,9},{25,17},{10,2},{18,10},{26,18},{... | collective-permute-start | bytes 1032200 | tf_op jit(solution)/shard_map/ppermute | solution.py:224
  12.9 14.4 %collective-permute-start.3 = (bf16[2,96,896]{2,1,0:T(8,128)(2,1)}, bf16[2,96,896]{2,1,0:T(8,128)(2,1)S(1)}, u32[]{:S(2)}, u32[]{:S(2)}) collective-permute-start(bf16[2,96,896]{2,1,0:T(8,128)(2,1)} %get-tuple-element.12), channel_id=1, source_target_pairs={{0,8},{8,16},{16,24},{1,9},{9,17},{17,25},{2,10},{10,18},{18,26},{... | collective-permute-start | bytes 1032200 | tf_op jit(solution)/shard_map/ppermute | solution.py:223
  17.5 10.8 %collective-permute-start.4 = (bf16[2,96,896]{2,1,0:T(8,128)(2,1)}, bf16[2,96,896]{2,1,0:T(8,128)(2,1)S(1)}, u32[]{:S(2)}, u32[]{:S(2)}) collective-permute-start(bf16[2,96,896]{2,1,0:T(8,128)(2,1)} %get-tuple-element.11), channel_id=1, source_target_pairs={{8,0},{16,8},{24,16},{9,1},{17,9},{25,17},{10,2},{18,10},{26,18},{... | collective-permute-start | bytes 1032200 | tf_op jit(solution)/shard_map/ppermute | solution.py:224
  26.8 13.9 %collective-permute-start.5 = (bf16[192,896]{1,0:T(8,128)(2,1)S(1)}, bf16[192,896]{1,0:T(8,128)(2,1)}, u32[]{:S(2)}, u32[]{:S(2)}) collective-permute-start(bf16[192,896]{1,0:T(8,128)(2,1)S(1)} %bitcast.93), channel_id=1, source_target_pairs={{0,1},{1,0},{2,3},{3,2},{4,5},{5,4},{6,7},{7,6},{8,9},{9,8},{10,11... | collective-permute-start | bytes 1032200 | tf_op jit(solution)/shard_map/ppermute | solution.py:142
  32.8 9.7 %collective-permute-start.6 = (bf16[192,896]{1,0:T(8,128)(2,1)S(1)}, bf16[192,896]{1,0:T(8,128)(2,1)S(1)}, u32[]{:S(2)}, u32[]{:S(2)}) collective-permute-start(bf16[192,896]{1,0:T(8,128)(2,1)S(1)} %bitcast.97), channel_id=1, source_target_pairs={{0,1},{1,0},{2,3},{3,2},{4,5},{5,4},{6,7},{7,6},{8,9},{9,8},{10,11... | collective-permute-start | bytes 1032200 | tf_op jit(solution)/shard_map/ppermute | solution.py:142
  33.5 10.6 %collective-permute-start.8 = (bf16[192,896]{1,0:T(8,128)(2,1)S(1)}, bf16[192,896]{1,0:T(8,128)(2,1)S(1)}, u32[]{:S(2)}, u32[]{:S(2)}) collective-permute-start(bf16[192,896]{1,0:T(8,128)(2,1)S(1)} %bitcast.98), channel_id=1, source_target_pairs={{0,2},{2,0},{4,6},{6,4},{1,3},{3,1},{5,7},{7,5},{8,10},{10,8},{12,... | collective-permute-start | bytes 1032200 | tf_op jit(solution)/shard_map/ppermute | solution.py:142
  35.1 26.6 %collective-permute-start.19 = (bf16[896,448]{0,1:T(8,128)(2,1)}, bf16[896,448]{0,1:T(8,128)(2,1)}, u32[]{:S(2)}, u32[]{:S(2)}) collective-permute-start(bf16[896,448]{0,1:T(8,128)(2,1)} %copy.21), channel_id=1, source_target_pairs={{0,8},{8,16},{16,24},{1,9},{9,17},{17,25},{2,10},{10,18},{18,26},{... | collective-permute-start | bytes 2408456 | tf_op jit(solution)/shard_map/ppermute | solution.py:201
  39.4 23.5 %collective-permute-start.22 = (bf16[896,448]{0,1:T(8,128)(2,1)}, bf16[896,448]{0,1:T(8,128)(2,1)}, u32[]{:S(2)}, u32[]{:S(2)}) collective-permute-start(bf16[896,448]{0,1:T(8,128)(2,1)} %copy.21), channel_id=1, source_target_pairs={{8,0},{16,8},{24,16},{9,1},{17,9},{25,17},{10,2},{18,10},{26,18},{... | collective-permute-start | bytes 2408456 | tf_op jit(solution)/shard_map/ppermute | solution.py:202
  42.5 11.1 %collective-permute-start.12 = (bf16[192,896]{1,0:T(8,128)(2,1)S(1)}, bf16[192,896]{1,0:T(8,128)(2,1)}, u32[]{:S(2)}, u32[]{:S(2)}) collective-permute-start(bf16[192,896]{1,0:T(8,128)(2,1)S(1)} %bitcast.99), channel_id=1, source_target_pairs={{0,4},{2,6},{4,0},{6,2},{1,5},{3,7},{5,1},{7,3},{8,12},{10,14},{12... | collective-permute-start | bytes 1032200 | tf_op jit(solution)/shard_map/ppermute | solution.py:142
  44.0 17.0 %collective-permute-start.11 = (bf16[192,896]{1,0:T(8,128)(2,1)S(1)}, bf16[192,896]{1,0:T(8,128)(2,1)}, u32[]{:S(2)}, u32[]{:S(2)}) collective-permute-start(bf16[192,896]{1,0:T(8,128)(2,1)S(1)} %bitcast.95), channel_id=1, source_target_pairs={{0,4},{2,6},{4,0},{6,2},{1,5},{3,7},{5,1},{7,3},{8,12},{10,14},{12... | collective-permute-start | bytes 1032200 | tf_op jit(solution)/shard_map/ppermute | solution.py:142
  44.7 18.8 %collective-permute-start.9 = (bf16[192,896]{1,0:T(8,128)(2,1)}, bf16[192,896]{1,0:T(8,128)(2,1)}, u32[]{:S(2)}, u32[]{:S(2)}) collective-permute-start(bf16[192,896]{1,0:T(8,128)(2,1)} %collective-permute-done.5), channel_id=1, source_target_pairs={{0,2},{2,0},{4,6},{6,4},{1,3},{3,1},{5,7},{7,5},{8,10},{10,8},{12,... | collective-permute-start | bytes 1032200 | tf_op jit(solution)/shard_map/ppermute | solution.py:142
  53.6 17.0 %collective-permute-start.13 = (bf16[192,896]{1,0:T(8,128)(2,1)}, bf16[192,896]{1,0:T(8,128)(2,1)}, u32[]{:S(2)}, u32[]{:S(2)}) collective-permute-start(bf16[192,896]{1,0:T(8,128)(2,1)} %collective-permute-done.5), channel_id=1, source_target_pairs={{0,4},{2,6},{4,0},{6,2},{1,5},{3,7},{5,1},{7,3},{8,12},{10,14},{12... | collective-permute-start | bytes 1032200 | tf_op jit(solution)/shard_map/ppermute | solution.py:142
  61.0 8.1 %collective-permute-start.14 = (bf16[192,896]{1,0:T(8,128)(2,1)}, bf16[192,896]{1,0:T(8,128)(2,1)}, u32[]{:S(2)}, u32[]{:S(2)}) collective-permute-start(bf16[192,896]{1,0:T(8,128)(2,1)} %collective-permute-done.12), channel_id=1, source_target_pairs={{0,1},{1,0},{2,3},{3,2},{4,5},{5,4},{6,7},{7,6},{8,9},{9,8},{10,11... | collective-permute-start | bytes 1032200 | tf_op jit(solution)/shard_map/ppermute | solution.py:142
  61.7 11.4 %collective-permute-start.10 = (bf16[192,896]{1,0:T(8,128)(2,1)S(1)}, bf16[192,896]{1,0:T(8,128)(2,1)}, u32[]{:S(2)}, u32[]{:S(2)}) collective-permute-start(bf16[192,896]{1,0:T(8,128)(2,1)S(1)} %collective-permute-done.6), channel_id=1, source_target_pairs={{0,2},{2,0},{4,6},{6,4},{1,3},{3,1},{5,7},{7,5},{8,10},{10,8},{12,... | collective-permute-start | bytes 1032200 | tf_op jit(solution)/shard_map/ppermute | solution.py:142
  62.9 11.8 %collective-permute-start.16 = (bf16[192,896]{1,0:T(8,128)(2,1)}, bf16[192,896]{1,0:T(8,128)(2,1)}, u32[]{:S(2)}, u32[]{:S(2)}) collective-permute-start(bf16[192,896]{1,0:T(8,128)(2,1)} %collective-permute-done.12), channel_id=1, source_target_pairs={{0,2},{2,0},{4,6},{6,4},{1,3},{3,1},{5,7},{7,5},{8,10},{10,8},{12,... | collective-permute-start | bytes 1032200 | tf_op jit(solution)/shard_map/ppermute | solution.py:142
  63.5 11.4 %collective-permute-start.15 = (bf16[192,896]{1,0:T(8,128)(2,1)}, bf16[192,896]{1,0:T(8,128)(2,1)}, u32[]{:S(2)}, u32[]{:S(2)}) collective-permute-start(bf16[192,896]{1,0:T(8,128)(2,1)} %collective-permute-done.11), channel_id=1, source_target_pairs={{0,2},{2,0},{4,6},{6,4},{1,3},{3,1},{5,7},{7,5},{8,10},{10,8},{12,... | collective-permute-start | bytes 1032200 | tf_op jit(solution)/shard_map/ppermute | solution.py:142
  69.1 7.6 %collective-permute-start.20 = (bf16[896,448]{0,1:T(8,128)(2,1)}, bf16[896,448]{0,1:T(8,128)(2,1)}, u32[]{:S(2)}, u32[]{:S(2)}) collective-permute-start(bf16[896,448]{0,1:T(8,128)(2,1)} %collective-permute-done.19), channel_id=1, source_target_pairs={{8,16},{16,24},{9,17},{17,25},{10,18},{18,26},{11,19},{19,27},{12,... | collective-permute-start | bytes 2408456 | tf_op jit(solution)/shard_map/ppermute | solution.py:201
  70.6 24.8 %collective-permute-start.23 = (bf16[896,448]{0,1:T(8,128)(2,1)}, bf16[896,448]{0,1:T(8,128)(2,1)}, u32[]{:S(2)}, u32[]{:S(2)}) collective-permute-start(bf16[896,448]{0,1:T(8,128)(2,1)} %collective-permute-done.22), channel_id=1, source_target_pairs={{8,0},{16,8},{9,1},{17,9},{10,2},{18,10},{11,3},{19,11},{12,4},{20... | collective-permute-start | bytes 2408456 | tf_op jit(solution)/shard_map/ppermute | solution.py:202
  76.7 41.5 %collective-permute-start.21 = (bf16[896,448]{0,1:T(8,128)(2,1)}, bf16[896,448]{0,1:T(8,128)(2,1)}, u32[]{:S(2)}, u32[]{:S(2)}) collective-permute-start(bf16[896,448]{0,1:T(8,128)(2,1)} %collective-permute-done.20), channel_id=1, source_target_pairs={{16,24},{17,25},{18,26},{19,27},{20,28},{21,29},{22,30},{23,31}} | collective-permute-start | bytes 2408456 | tf_op jit(solution)/shard_map/ppermute | solution.py:201
  95.4 25.1 %collective-permute-start.24 = (bf16[896,448]{0,1:T(8,128)(2,1)}, bf16[896,448]{0,1:T(8,128)(2,1)}, u32[]{:S(2)}, u32[]{:S(2)}) collective-permute-start(bf16[896,448]{0,1:T(8,128)(2,1)} %collective-permute-done.23), channel_id=1, source_target_pairs={{8,0},{9,1},{10,2},{11,3},{12,4},{13,5},{14,6},{15,7}} | collective-permute-start | bytes 2408456 | tf_op jit(solution)/shard_map/ppermute | solution.py:202
  148.1 14.1 %collective-permute-start.28 = (bf16[2,96,448]{2,1,0:T(8,128)(2,1)S(1)}, bf16[2,96,448]{2,1,0:T(8,128)(2,1)S(1)}, u32[]{:S(2)}, u32[]{:S(2)}) collective-permute-start(bf16[2,96,448]{2,1,0:T(8,128)(2,1)S(1)} %select_bitcast_fusion), channel_id=1, source_target_pairs={{0,1},{1,0},{2,3},{3,2},{4,5},{5,4},{6,7},{7,6},{8,9},{9,8},{10,11... | collective-permute-start | bytes 516104 | tf_op jit(solution)/shard_map/ppermute | solution.py:142
  149.9 11.6 %collective-permute-start.34 = (f32[448]{0:T(512)S(1)}, f32[448]{0:T(512)S(1)}, u32[]{:S(2)}, u32[]{:S(2)}) collective-permute-start(f32[448]{0:T(512)S(1)} %slice_multiply_fusion), channel_id=1, source_target_pairs={{0,1},{1,0},{2,3},{3,2},{4,5},{5,4},{6,7},{7,6},{8,9},{9,8},{10,11... | collective-permute-start | bytes 5384 | tf_op jit(solution)/shard_map/ppermute | solution.py:142
  (30 other events, 113.1 us)
where the time goes:
time: 165 us; the launch traced here: 164 us
  waiting for transfers between devices  47.8 us (29%)
  starting transfers between devices  46.6 us (28%)
  local copies, waits for them, and re-layouts  32.6 us (20%)
  Pallas kernels  18.5 us (11%)
  other arithmetic  15.3 us (9%)
  between operations  3.49 us (2%)
    ppermute x25, waiting for transfers between devices, swap(): return lax.ppermute(array, axis, [(i, i ^ distance) for i in range(count)])  28.2 us
    ppermute x25, starting transfers between devices, swap(): return lax.ppermute(array, axis, [(i, i ^ distance) for i in range(count)])  24.7 us
    ppermute x3, waiting for transfers between devices, local(): falling = lax.ppermute(falling, 'frames', down[:slab_count - step])  17.1 us
    unnamed x38, local copies, waits for them, and re-layouts  14 us
    pallas_call x2, Pallas kernels, project(): pl.pallas_call(kernel, grid_spec=pltpu.PrefetchScalarGridSpec(num_scalar_...  9.48 us
    pallas_call x2, Pallas kernels, attention(): pl.pallas_call(attend_kernel, grid_spec=pltpu.PrefetchScalarGridSpec(num_...  9 us
    ppermute x2, starting transfers between devices, local(): left = lax.ppermute(stream[slots - 1, 1:], 'frames', up)  8.04 us
    ppermute x3, starting transfers between devices, local(): rising = lax.ppermute(rising, 'frames', up[step - 1:])  7.51 us
  transfers between devices with their start and end apart: 35, of which 14 were waited for; matrix products, arithmetic and copies ran while one was open for 18% of the time, Pallas kernels for 9%

commit v1 on v0

--- a/solution.py
+++ b/solution.py
@@ -68,9 +68,9 @@
             out_specs=pl.BlockSpec((slots, tile_len, block), lambda h, c: (0, 0, h)),
         ),
         out_shape=jax.ShapeDtypeStruct((slots, tile_len, width), jnp.bfloat16),
-        compiler_params=pltpu.CompilerParams(vmem_limit_bytes=24 * 1024 * 1024),
+        compiler_params=pltpu.CompilerParams(vmem_limit_bytes=48 * 1024 * 1024),
         cost_estimate=pl.CostEstimate(
-            flops=16 * slots * tile_len * tile_len * width,
+            flops=300 * slots * tile_len * tile_len * width,
             bytes_accessed=12 * slots * tile_len * width,
             transcendentals=0,
         ),
@@ -78,56 +78,86 @@
     )(nearby, own, left, right)
 
 
-def project_kernel(shard_total, with_total, places_ref, *refs):
-    rows_ref = refs[0]
-    weight_refs = refs[1 : 1 + shard_total]
-    out_ref = refs[-1]
-    shard = pl.program_id(1)
-
-    def add(weight_ref, first):
-        term = jnp.dot(
-            rows_ref[0, 0], weight_ref[...], preferred_element_type=jnp.float32
-        )
-        if not first:
-            out_ref[0] = out_ref[0] + term
-        elif with_total:
-            out_ref[0] = refs[1 + shard_total][0] + term
+def project(places, valid, clip_index, blocks, weights, total):
+    clip_count, stream_count = len(blocks[0]), len(blocks[0][0])
+    block_rows, depth = blocks[0][0][0].shape
+    columns = weights[0].shape[0]
+    row_count = stream_count * block_rows
+    shard_total = len(weights)
+    scalars = jnp.stack([jnp.int32(n) for n in (*places, *valid, clip_index)])
+    flat = [block for place in blocks for clip in place for block in clip]
+
+    def kernel(scalars_ref, *refs):
+        block_refs = refs[: len(flat)]
+        weight_refs = refs[len(flat) : len(flat) + shard_total]
+        total_ref = refs[len(flat) + shard_total] if total is not None else None
+        out_ref, rows, held, row_sem, weight_sem = refs[-5:]
+
+        def weight_copy(shard):
+            return pltpu.make_async_copy(weight_refs[shard], held.at[shard], weight_sem.at[shard])
+
+        def row_copy(place, shard, clip, stream):
+            source = block_refs[(place * clip_count + clip) * stream_count + stream]
+            first = pl.multiple_of(
+                (clip ^ scalars_ref[2 * shard_total]) * row_count + stream * block_rows, 16
+            )
+            return pltpu.make_async_copy(
+                source,
+                rows.at[shard, pl.ds(first, block_rows)],
+                row_sem.at[shard, clip, stream],
+            )
+
+        for shard in range(shard_total):
+
+            @pl.when(scalars_ref[shard_total + shard] == 1)
+            def _():
+                weight_copy(shard).start()
+                for place in range(len(blocks)):
+
+                    @pl.when(scalars_ref[shard] == place)
+                    def _():
+                        for clip in range(clip_count):
+                            for stream in range(stream_count):
+                                row_copy(place, shard, clip, stream).start()
+
+        if total is not None:
+            out_ref[...] = total_ref[...]
         else:
-            out_ref[0] = term
-
-    for n in range(shard_total):
-        pl.when(shard == n)(lambda n=n: add(weight_refs[n], n == 0))
-
-
-def project(places, clip_index, rows, weights, total):
-    _, clip_count, row_count, depth = rows.shape
-    columns = weights[0].shape[1]
-    shard_total = len(weights)
-    scalars = jnp.concatenate([jnp.stack(places), clip_index[None]]).astype(jnp.int32)
-    out_spec = pl.BlockSpec((1, row_count, columns), lambda c, j, s: (c, 0, 0))
-    operands = [rows, *weights]
-    in_specs = [
-        pl.BlockSpec(
-            (1, 1, row_count, depth), lambda c, j, s: (s[j], c ^ s[shard_total], 0, 0)
-        )
-    ] + [pl.BlockSpec((depth, columns), lambda c, j, s: (0, 0)) for _ in weights]
+            out_ref[...] = jnp.zeros_like(out_ref)
+
+        for shard in range(shard_total):
+
+            @pl.when(scalars_ref[shard_total + shard] == 1)
+            def _():
+                weight_copy(shard).wait()
+                for clip in range(clip_count):
+                    for stream in range(stream_count):
+                        row_copy(0, shard, clip, stream).wait()
+                for clip in range(clip_count):
+                    out_ref[clip] += lax.dot_general(
+                        rows[shard, pl.ds(clip * row_count, row_count)],
+                        held[shard],
+                        (((1,), (1,)), ((), ())),
+                        preferred_element_type=jnp.float32,
+                    )
+
+    operands = [*flat, *weights]
+    in_specs = [pl.BlockSpec(memory_space=pl.ANY) for _ in operands]
     if total is not None:
         operands.append(total)
-        in_specs.append(out_spec)
-
-    def kernel(*refs):
-        project_kernel(shard_total, total is not None, *refs)
-
+        in_specs.append(pl.BlockSpec(memory_space=pltpu.VMEM))
     return pl.pallas_call(
         kernel,
-        grid_spec=pltpu.PrefetchScalarGridSpec(
-            num_scalar_prefetch=1,
-            grid=(clip_count, shard_total),
-            in_specs=in_specs,
-            out_specs=out_spec,
-        ),
+        in_specs=[pl.BlockSpec(memory_space=pltpu.SMEM)] + in_specs,
+        out_specs=pl.BlockSpec(memory_space=pltpu.VMEM),
         out_shape=jax.ShapeDtypeStruct((clip_count, row_count, columns), jnp.float32),
-        compiler_params=pltpu.CompilerParams(vmem_limit_bytes=40 * 1024 * 1024),
+        scratch_shapes=[
+            pltpu.VMEM((shard_total, clip_count * row_count, depth), jnp.bfloat16),
+            pltpu.VMEM((shard_total, columns, depth), jnp.bfloat16),
+            pltpu.SemaphoreType.DMA((shard_total, clip_count, stream_count)),
+            pltpu.SemaphoreType.DMA((shard_total,)),
+        ],
+        compiler_params=pltpu.CompilerParams(vmem_limit_bytes=56 * 1024 * 1024),
         cost_estimate=pl.CostEstimate(
             flops=2 * clip_count * row_count * depth * columns * shard_total,
             bytes_accessed=shard_total * depth * (clip_count * row_count + columns) * 2,
@@ -156,10 +186,9 @@
     return blocks
 
 
-def add_up(array, order):
-    for axis, distance in order:
-        array = array + swap(array, axis, distance)
-    return array
+def collect(array, axes):
+    copies = jnp.broadcast_to(array[None], (lax.axis_size(axes),) + array.shape)
+    return lax.all_to_all(copies, axes, split_axis=0, concat_axis=0, tiled=True)
 
 
 def pick(options, index):
@@ -192,8 +221,8 @@
     up = [(i, i + 1) for i in range(slab_count - 1)]
     down = [(i + 1, i) for i in range(slab_count - 1)]
 
-    own_weight = own_columns(out_weight)
-    shards = [(own_weight, slab_index)]
+    own_weight = own_columns(out_weight).T
+    shards = [(own_weight, slab_index, jnp.int32(1))]
     line = slab_count == model_count
     if line:
         rising = falling = own_weight
@@ -201,8 +230,12 @@
             rising = lax.ppermute(rising, "frames", up[step - 1 :])
             falling = lax.ppermute(falling, "frames", down[: slab_count - step])
             shards += [
-                (rising, jnp.maximum(slab_index - step, 0)),
-                (falling, jnp.minimum(slab_index + step, slab_count - 1)),
+                (rising, jnp.maximum(slab_index - step, 0), slab_index >= step),
+                (
+                    falling,
+                    jnp.minimum(slab_index + step, slab_count - 1),
+                    slab_index < slab_count - step,
+                ),
             ]
 
     spread_counts = spread(live_counts[0], distances("dp"))
@@ -224,48 +257,37 @@
         right = lax.ppermute(stream[0, 1:], "frames", down)
         attended = attention(nearby, stream, left, right)
         gathered.append(spread(attended.reshape(near_rows, local_width), order))
-    rows = jnp.stack(
-        [
-            jnp.stack(
-                [jnp.concatenate([g[m, c] for g in gathered], axis=0) for c in range(clip_count)]
+    blocks = [
+        [[g[m, c] for g in gathered] for c in range(clip_count)] for m in range(model_count)
+    ]
+
+    def project_shards(some, total):
+        return project(
+            [place ^ model_index for _, place, _ in some],
+            [exists for _, _, exists in some],
+            clip_index,
+            blocks,
+            [weight for weight, _, _ in some],
+            total,
+        )
+
+    if line:
+        total = project_shards(shards[:-2], None)
+        total = project_shards(shards[-2:], total)
+    else:
+        weight = lax.all_gather(own_weight, "frames", axis=1, tiled=True)
+        shards = [
+            (
+                lax.dynamic_slice_in_dim(weight, m * local_width, local_width, axis=1),
+                jnp.int32(m),
+                jnp.int32(1),
             )
             for m in range(model_count)
         ]
-    )
-
-    if line:
-        early, late = shards[:-2], shards[-2:]
-        total = project(
-            [place ^ model_index for _, place in early],
-            clip_index,
-            rows,
-            [weight for weight, _ in early],
-            None,
-        )
-        total = project(
-            [place ^ model_index for _, place in late],
-            clip_index,
-            rows,
-            [weight for weight, _ in late],
-            total,
-        )
-    else:
-        weight = lax.all_gather(own_weight, "frames", axis=0, tiled=True)
-        weight = weight.reshape(model_count, local_width, half)
-        total = project(
-            [jnp.int32(m) for m in range(model_count)],
-            clip_index,
-            rows,
-            [
-                lax.dynamic_index_in_dim(weight, model_index ^ m, 0, keepdims=False)
-                for m in range(model_count)
-            ],
-            None,
-        )
+        total = project_shards(shards, None)
     projected = total.reshape(clip_count, 2, slots, tile_len, half)
 
-    everyone = distances("dp") + distances("mp")
-    squares = add_up(jnp.sum(projected * projected, axis=-1), everyone)
+    squares = jnp.sum(collect(jnp.sum(projected * projected, axis=-1), ("mp", "dp")), axis=0)
     scale = lax.rsqrt(squares / model_width + epsilon)[..., None]
     own_counts = jnp.stack([n[1 : slots + 1] for n in near_counts])
     live = (jnp.arange(tile_len) < own_counts[..., None]).astype(jnp.float32)[..., None]
@@ -289,18 +311,14 @@
     )[None]
 
     sums = jnp.concatenate([jnp.sum(feature_sums, axis=0), penalties])
-    sums = add_up(sums, distances("frames"))
-    gain_halves = spread(sums[:half] * gain, distances("dp"))
-    gain_grad = jnp.concatenate(
-        [
-            pick([gain_halves[0, n ^ d] for d in range(clip_count)], clip_index)
-            for n in range(clip_count)
-        ]
-    ) / (sigma_noise * sigma_noise * token_total)
-    penalties = add_up(sums[half:], everyone)
+    sums = collect(sums, ("frames", "mp", "dp"))
+    penalties = jnp.sum(sums[:, half:], axis=0)
     penalty = pick([penalties[d : d + 1] for d in range(clip_count)], clip_index) / (
         sigma_noise * sigma_noise * token_total * model_width
     )
+    sums = sums[:, :half].reshape(slab_count, model_count, local_width)
+    sums = lax.dynamic_index_in_dim(jnp.sum(sums, axis=0), model_index, 0, keepdims=False)
+    gain_grad = norm_gain * sums / (sigma_noise * sigma_noise * token_total)
     return (features, penalty, gain_grad)
 
 

time: 165 us -> 144 us (0.87)
  local copies, waits for them, and re-layouts: 32.6 us -> 8.81 us
  waiting for transfers between devices: 47.8 us -> 62.2 us
  other arithmetic: 15.3 us -> 5.63 us
  starting transfers between devices: 46.6 us -> 42.2 us
  Pallas kernels: 18.5 us -> 20.8 us
    ppermute x6 -> x0, local copies, waits for them, and re-layouts: 13.5 us -> none  [the longest x3 6.79 us: local(): falling = lax.ppermute(falling, 'frames', down[:slab_count - step])]
    ppermute x25 -> x16, starting transfers between devices: 24.7 us -> 12.3 us  [swap(): return lax.ppermute(array, axis, [(i, i ^ distance) for i in range(count)])]
    unnamed x38 -> x39, local copies, waits for them, and re-layouts: 14 us -> 2.59 us
    all_to_all x0 -> x2, waiting for transfers between devices: none -> 10.5 us  [collect(): return lax.all_to_all(copies, axes, split_axis=0, concat_axis=0, tiled=True)]
    another operation x13 -> x0, other arithmetic: 10.4 us -> none  [the longest x8 6.73 us: local(): jnp.stack([jnp.concatenate([g[m, c] for g in gathered], axis=0) for c in...]
    ppermute x2, waiting for transfers between devices: 0.01 us -> 10.3 us  [local(): left = lax.ppermute(stream[slots - 1, 1:], 'frames', up)]
    ppermute x25 -> x16, waiting for transfers between devices: 28.2 us -> 18.7 us  [swap(): return lax.ppermute(array, axis, [(i, i ^ distance) for i in range(count)])]
    all_to_all x0 -> x2, starting transfers between devices: none -> 6.29 us  [collect(): return lax.all_to_all(copies, axes, split_axis=0, concat_axis=0, tiled=True)]
  transfers between devices with their start and end apart: 35 -> 28, of which waited for: 14 -> 12; matrix products, arithmetic and copies ran while one was open for 18% -> 3% of each run, Pallas kernels for 9% -> 11%
where the time goes in v1:
time: 144 us; the launch traced here: 143 us
  waiting for transfers between devices  62.2 us (43%)
  starting transfers between devices  42.2 us (29%)
  Pallas kernels  20.8 us (14%)
  local copies, waits for them, and re-layouts  8.81 us (6%)
  other arithmetic  5.63 us (4%)
  between operations  3.48 us (2%)
    ppermute x3, waiting for transfers between devices, local(): falling = lax.ppermute(falling, 'frames', down[:slab_count - step])  18.9 us
    ppermute x16, waiting for transfers between devices, swap(): return lax.ppermute(array, axis, [(i, i ^ distance) for i in range(count)])  18.7 us
    ppermute x16, starting transfers between devices, swap(): return lax.ppermute(array, axis, [(i, i ^ distance) for i in range(count)])  12.3 us
    pallas_call x2, Pallas kernels, project(): pl.pallas_call(kernel, in_specs=[pl.BlockSpec(memory_space=pltpu.SMEM)] +...  11.8 us
    all_to_all x2, waiting for transfers between devices, collect(): return lax.all_to_all(copies, axes, split_axis=0, concat_axis=0, tiled=True)  10.5 us
    ppermute x2, waiting for transfers between devices, local(): left = lax.ppermute(stream[slots - 1, 1:], 'frames', up)  10.3 us
    ppermute x2, starting transfers between devices, local(): left = lax.ppermute(stream[slots - 1, 1:], 'frames', up)  9.12 us
    pallas_call x2, Pallas kernels, attention(): pl.pallas_call(attend_kernel, grid_spec=pltpu.PrefetchScalarGridSpec(num_...  9 us
  transfers between devices with their start and end apart: 28, of which 12 were waited for; matrix products, arithmetic and copies ran while one was open for 3% of the time, Pallas kernels for 11%

profile of v1, /device:TPU:0, one launch (start us, length us, event | category | flops | bytes accessed | tf_op | source)
XLA Modules:
  0.0 143.1 jit_solution(8782131227960007310)
XLA Ops:
  0.6 1.9 %fusion.6 = (bf16[896,448]{1,0:T(8,128)(2,1)S(1)}, bf16[896,448]{1,0:T(8,128)(2,1)S(1)}) fusion(bf16[896,896]{1,0:T(8,128)(2,1)} %param.7), kind=kLoop, calls=%fused_computation.39 | loop fusion | bytes 3211264 | tf_op jit(solution)/shard_map/slice | solution.py:215
  5.2 5.8 %collective-permute-start.19 = (bf16[448,896]{1,0:T(8,128)(2,1)}, bf16[448,896]{1,0:T(8,128)(2,1)}, u32[]{:S(2)}, u32[]{:S(2)}) collective-permute-start(bf16[448,896]{1,0:T(8,128)(2,1)} %select_bitcast_fusion.refs_16_), channel_id=1, source_target_pairs={{0,8},{8,16},{16,24},{1,9},{9,17},{17,25},{2,10},{10,18},{18,26},{... | collective-permute-start | bytes 2408456 | tf_op jit(solution)/shard_map/ppermute | solution.py:230
  12.3 1.6 %collective-permute-start = (s32[8]{0:T(128)S(1)}, s32[8]{0:T(128)S(1)}, u32[]{:S(2)}, u32[]{:S(2)}) collective-permute-start(s32[8]{0:T(128)S(1)} %bitcast.93), channel_id=1, source_target_pairs={{0,1},{1,0},{2,3},{3,2},{4,5},{5,4},{6,7},{7,6},{8,9},{9,8},{10,11... | collective-permute-start | bytes 104 | tf_op jit(solution)/shard_map/ppermute | solution.py:172
  15.2 4.6 %collective-permute-start.3 = (bf16[2,96,896]{2,1,0:T(8,128)(2,1)}, bf16[2,96,896]{2,1,0:T(8,128)(2,1)S(1)}, u32[]{:S(2)}, u32[]{:S(2)}) collective-permute-start(bf16[2,96,896]{2,1,0:T(8,128)(2,1)} %get-tuple-element.12), channel_id=1, source_target_pairs={{0,8},{8,16},{16,24},{1,9},{9,17},{17,25},{2,10},{10,18},{18,26},{... | collective-permute-start | bytes 1032200 | tf_op jit(solution)/shard_map/ppermute | solution.py:256
  21.1 4.6 %collective-permute-start.1 = (bf16[2,96,896]{2,1,0:T(8,128)(2,1)S(1)}, bf16[2,96,896]{2,1,0:T(8,128)(2,1)S(1)}, u32[]{:S(2)}, u32[]{:S(2)}) collective-permute-start(bf16[2,96,896]{2,1,0:T(8,128)(2,1)S(1)} %get-tuple-element.14), channel_id=1, source_target_pairs={{0,8},{8,16},{16,24},{1,9},{9,17},{17,25},{2,10},{10,18},{18,26},{... | collective-permute-start | bytes 1032200 | tf_op jit(solution)/shard_map/ppermute | solution.py:256
  25.8 10.3 %collective-permute-done.3.left_ref = bf16[2,96,896]{2,1,0:T(8,128)(2,1)S(1)} collective-permute-done((bf16[2,96,896]{2,1,0:T(8,128)(2,1)}, bf16[2,96,896]{2,1,0:T(8,128)(2,1)S(1)}, u32[]{:S(2)}, u32[]{:S(2)}) %collective-permute-start.3) | collective-permute-done | bytes 344096 | tf_op jit(solution)/shard_map/ppermute | solution.py:256
  37.4 3.2 %collective-permute-done.4.right_ref = bf16[2,96,896]{2,1,0:T(8,128)(2,1)S(1)} collective-permute-done((bf16[2,96,896]{2,1,0:T(8,128)(2,1)}, bf16[2,96,896]{2,1,0:T(8,128)(2,1)S(1)}, u32[]{:S(2)}, u32[]{:S(2)}) %collective-permute-start.4) | collective-permute-done | bytes 344096 | tf_op jit(solution)/shard_map/ppermute | solution.py:257
  40.6 4.5 %attention.3 = bf16[2,96,896]{2,1,0:T(8,128)(2,1)S(1)} custom-call(s32[4]{0:T(128)S(1)} %get-tuple-element.5.counts_ref, bf16[2,3,96,896]{3,2,1,0:T(8,128)(2,1)S(1)} %fusion.own_ref, bf16[2,96,896]{2,1,0:T(8,128)(2,1)S(1)} %collective-permute-done.3.left_ref, bf16[2,96,896]{2,1,0:T(8,128)(2,1)S(1)} %collective-permute-done.4.right_ref), custom_call_target="tpu_custom_call" | custom-call | flops 4954521600 | bytes 2064384 | tf_op jit(solution)/shard_map/attention/pallas_call | solution.py:62
  47.2 4.5 %attention.2 = bf16[2,96,896]{2,1,0:T(8,128)(2,1)S(1)} custom-call(s32[4]{0:T(128)S(1)} %get-tuple-element.5.counts_ref, bf16[2,3,96,896]{3,2,1,0:T(8,128)(2,1)S(1)} %bitcast.79, bf16[2,96,896]{2,1,0:T(8,128)(2,1)S(1)} %collective-permute-done.1.left_ref, bf16[2,96,896]{2,1,0:T(8,128)(2,1)S(1)} %collective-permute-done.2.right_ref), custom_call_target="tpu_custom_call" | custom-call | flops 4954521600 | bytes 2064384 | tf_op jit(solution)/shard_map/attention/pallas_call | solution.py:62
  51.7 1.6 %collective-permute-start.5 = (bf16[192,896]{1,0:T(8,128)(2,1)S(1)}, bf16[192,896]{1,0:T(8,128)(2,1)S(1)}, u32[]{:S(2)}, u32[]{:S(2)}) collective-permute-start(bf16[192,896]{1,0:T(8,128)(2,1)S(1)} %bitcast.85), channel_id=1, source_target_pairs={{0,1},{1,0},{2,3},{3,2},{4,5},{5,4},{6,7},{7,6},{8,9},{9,8},{10,11... | collective-permute-start | bytes 1032200 | tf_op jit(solution)/shard_map/ppermute | solution.py:172
  55.3 7.5 %collective-permute-done.5.refs_2_ = bf16[192,896]{1,0:T(8,128)(2,1)S(1)} collective-permute-done((bf16[192,896]{1,0:T(8,128)(2,1)S(1)}, bf16[192,896]{1,0:T(8,128)(2,1)S(1)}, u32[]{:S(2)}, u32[]{:S(2)}) %collective-permute-start.5) | collective-permute-done | bytes 344096 | tf_op jit(solution)/shard_map/ppermute | solution.py:172
  62.8 1.6 %collective-permute-start.20 = (bf16[448,896]{1,0:T(8,128)(2,1)}, bf16[448,896]{1,0:T(8,128)(2,1)}, u32[]{:S(2)}, u32[]{:S(2)}) collective-permute-start(bf16[448,896]{1,0:T(8,128)(2,1)} %collective-permute-done.19.refs_17_), channel_id=1, source_target_pairs={{8,16},{16,24},{9,17},{17,25},{10,18},{18,26},{11,19},{19,27},{12,... | collective-permute-start | bytes 2408456 | tf_op jit(solution)/shard_map/ppermute | solution.py:230
  67.2 1.6 %collective-permute-start.14 = (bf16[192,896]{1,0:T(8,128)(2,1)S(1)}, bf16[192,896]{1,0:T(8,128)(2,1)}, u32[]{:S(2)}, u32[]{:S(2)}) collective-permute-start(bf16[192,896]{1,0:T(8,128)(2,1)S(1)} %collective-permute-done.12.refs_9_), channel_id=1, source_target_pairs={{0,1},{1,0},{2,3},{3,2},{4,5},{5,4},{6,7},{7,6},{8,9},{9,8},{10,11... | collective-permute-start | bytes 1032200 | tf_op jit(solution)/shard_map/ppermute | solution.py:172
  70.2 7.5 %collective-permute-done.14.refs_11_ = bf16[192,896]{1,0:T(8,128)(2,1)} collective-permute-done((bf16[192,896]{1,0:T(8,128)(2,1)S(1)}, bf16[192,896]{1,0:T(8,128)(2,1)}, u32[]{:S(2)}, u32[]{:S(2)}) %collective-permute-start.14) | collective-permute-done | bytes 344096 | tf_op jit(solution)/shard_map/ppermute | solution.py:172
  81.5 6.7 %collective-permute-done.23.refs_20_ = bf16[448,896]{1,0:T(8,128)(2,1)} collective-permute-done((bf16[448,896]{1,0:T(8,128)(2,1)}, bf16[448,896]{1,0:T(8,128)(2,1)}, u32[]{:S(2)}, u32[]{:S(2)}) %collective-permute-start.23) | collective-permute-done | bytes 802848 | tf_op jit(solution)/shard_map/ppermute | solution.py:231
  90.9 6.6 %project.2.refs_18_ = f32[2,384,448]{2,1,0:T(8,128)} custom-call(s32[11]{0:T(128)} %stack.97.scalars_ref, bf16[192,896]{1,0:T(8,128)(2,1)} %bitcast.88, bf16[192,896]{1,0:T(8,128)(2,1)} %bitcast.83, bf16[192,896]{1,0:T(8,128)(2,1)} %copy-done.8, bf16[192,896]{1,0:T(8,128)(2,1)} %copy-done.9, bf16[192,896]{1,0:T(8,128)(2,1)} %copy-done.12, ...), custom_call_target="tpu_custom_call" | custom-call | flops 3082813440 | bytes 10895360 | tf_op jit(solution)/shard_map/project/pallas_call | solution.py:149
  97.6 12.2 %collective-permute-done.24.refs_17_ = bf16[448,896]{1,0:T(8,128)(2,1)S(1)} collective-permute-done((bf16[448,896]{1,0:T(8,128)(2,1)}, bf16[448,896]{1,0:T(8,128)(2,1)S(1)}, u32[]{:S(2)}, u32[]{:S(2)}) %collective-permute-start.24) | collective-permute-done | bytes 802848 | tf_op jit(solution)/shard_map/ppermute | solution.py:231
  110.7 5.2 %project.3 = f32[2,384,448]{2,1,0:T(8,128)} custom-call(s32[5]{0:T(128)} %stack.83.scalars_ref, bf16[192,896]{1,0:T(8,128)(2,1)} %bitcast.89, bf16[192,896]{1,0:T(8,128)(2,1)} %bitcast.84, bf16[192,896]{1,0:T(8,128)(2,1)} %copy-done.8, bf16[192,896]{1,0:T(8,128)(2,1)} %copy-done.9, bf16[192,896]{1,0:T(8,128)(2,1)} %copy-done.12, ...), custom_call_target="tpu_custom_call" | custom-call | flops 1233125376 | bytes 4358144 | tf_op jit(solution)/shard_map/project/pallas_call | solution.py:149
  115.9 1.7 %multiply_reduce_fusion = f32[2,384]{1,0:T(2,128)S(1)} fusion(f32[2,384,448]{2,1,0:T(8,128)} %project.3), kind=kLoop, calls=%fused_computation.3 | loop fusion | flops 687360 | bytes 1379328 | tf_op jit(solution)/shard_map/reduce_sum | solution.py:290
  118.3 3.7 %all-to-all-start = ((f32[8,2,2,2,96]{4,3,2,1,0:T(2,128)}), f32[8,2,2,2,96]{4,3,2,1,0:T(2,128)S(1)}, u32[]{:S(2)}, u32[]{:S(2)}) async-start(f32[8,2,2,2,96]{4,3,2,1,0:T(2,128)} %broadcast_in_dim.9), calls=%async_computation | async-start | bytes 65536 | tf_op jit(solution)/shard_map/all_to_all | solution.py:191
  122.1 4.6 %all-to-all-done = f32[8,2,2,2,96]{4,3,2,1,0:T(2,128)S(1)} async-done(((f32[8,2,2,2,96]{4,3,2,1,0:T(2,128)}), f32[8,2,2,2,96]{4,3,2,1,0:T(2,128)S(1)}, u32[]{:S(2)}, u32[]{:S(2)}) %all-to-all-start) | async-done | bytes 24608 | tf_op jit(solution)/shard_map/all_to_all | solution.py:191
  128.2 2.6 %all-to-all-start.1 = ((f32[32,1,450]{2,1,0:T(1,128)}), f32[32,1,450]{2,1,0:T(1,128)S(1)}, u32[]{:S(2)}, u32[]{:S(2)}) async-start(f32[32,1,450]{2,1,0:T(1,128)} %broadcast_in_dim.11), calls=%async_computation.1 | async-start | bytes 131072 | tf_op jit(solution)/shard_map/all_to_all | solution.py:191
  130.8 1.7 %collective-permute-start.25 = (bf16[2,96,448]{2,1,0:T(8,128)(2,1)S(1)}, bf16[2,96,448]{2,1,0:T(8,128)(2,1)S(1)}, u32[]{:S(2)}, u32[]{:S(2)}) collective-permute-start(bf16[2,96,448]{2,1,0:T(8,128)(2,1)S(1)} %select_bitcast_fusion.1), channel_id=1, source_target_pairs={{0,1},{1,0},{2,3},{3,2},{4,5},{5,4},{6,7},{7,6},{8,9},{9,8},{10,11... | collective-permute-start | bytes 516104 | tf_op jit(solution)/shard_map/ppermute | solution.py:172
  132.5 5.9 %all-to-all-done.1 = f32[32,1,450]{2,1,0:T(1,128)S(1)} async-done(((f32[32,1,450]{2,1,0:T(1,128)}), f32[32,1,450]{2,1,0:T(1,128)S(1)}, u32[]{:S(2)}, u32[]{:S(2)}) %all-to-all-start.1) | async-done | bytes 57632 | tf_op jit(solution)/shard_map/all_to_all | solution.py:191
  (106 shorter events, 28.0 us)
Async XLA Ops:
  5.2 57.6 %collective-permute-start.19 = (bf16[448,896]{1,0:T(8,128)(2,1)}, bf16[448,896]{1,0:T(8,128)(2,1)}, u32[]{:S(2)}, u32[]{:S(2)}) collective-permute-start(bf16[448,896]{1,0:T(8,128)(2,1)} %select_bitcast_fusion.refs_16_), channel_id=1, source_target_pairs={{0,8},{8,16},{16,24},{1,9},{9,17},{17,25},{2,10},{10,18},{18,26},{... | collective-permute-start | bytes 2408456 | tf_op jit(solution)/shard_map/ppermute | solution.py:230
  11.0 53.4 %collective-permute-start.22 = (bf16[448,896]{1,0:T(8,128)(2,1)}, bf16[448,896]{1,0:T(8,128)(2,1)}, u32[]{:S(2)}, u32[]{:S(2)}) collective-permute-start(bf16[448,896]{1,0:T(8,128)(2,1)} %select_bitcast_fusion.refs_16_), channel_id=1, source_target_pairs={{8,0},{16,8},{24,16},{9,1},{17,9},{25,17},{10,2},{18,10},{26,18},{... | collective-permute-start | bytes 2408456 | tf_op jit(solution)/shard_map/ppermute | solution.py:231
  12.3 8.8 %collective-permute-start = (s32[8]{0:T(128)S(1)}, s32[8]{0:T(128)S(1)}, u32[]{:S(2)}, u32[]{:S(2)}) collective-permute-start(s32[8]{0:T(128)S(1)} %bitcast.93), channel_id=1, source_target_pairs={{0,1},{1,0},{2,3},{3,2},{4,5},{5,4},{6,7},{7,6},{8,9},{9,8},{10,11... | collective-permute-start | bytes 104 | tf_op jit(solution)/shard_map/ppermute | solution.py:172
  15.2 21.0 %collective-permute-start.3 = (bf16[2,96,896]{2,1,0:T(8,128)(2,1)}, bf16[2,96,896]{2,1,0:T(8,128)(2,1)S(1)}, u32[]{:S(2)}, u32[]{:S(2)}) collective-permute-start(bf16[2,96,896]{2,1,0:T(8,128)(2,1)} %get-tuple-element.12), channel_id=1, source_target_pairs={{0,8},{8,16},{16,24},{1,9},{9,17},{17,25},{2,10},{10,18},{18,26},{... | collective-permute-start | bytes 1032200 | tf_op jit(solution)/shard_map/ppermute | solution.py:256
  19.7 20.9 %collective-permute-start.4 = (bf16[2,96,896]{2,1,0:T(8,128)(2,1)}, bf16[2,96,896]{2,1,0:T(8,128)(2,1)S(1)}, u32[]{:S(2)}, u32[]{:S(2)}) collective-permute-start(bf16[2,96,896]{2,1,0:T(8,128)(2,1)} %get-tuple-element.11), channel_id=1, source_target_pairs={{8,0},{16,8},{24,16},{9,1},{17,9},{25,17},{10,2},{18,10},{26,18},{... | collective-permute-start | bytes 1032200 | tf_op jit(solution)/shard_map/ppermute | solution.py:257
  21.1 25.6 %collective-permute-start.1 = (bf16[2,96,896]{2,1,0:T(8,128)(2,1)S(1)}, bf16[2,96,896]{2,1,0:T(8,128)(2,1)S(1)}, u32[]{:S(2)}, u32[]{:S(2)}) collective-permute-start(bf16[2,96,896]{2,1,0:T(8,128)(2,1)S(1)} %get-tuple-element.14), channel_id=1, source_target_pairs={{0,8},{8,16},{16,24},{1,9},{9,17},{17,25},{2,10},{10,18},{18,26},{... | collective-permute-start | bytes 1032200 | tf_op jit(solution)/shard_map/ppermute | solution.py:256
  36.1 11.1 %collective-permute-start.2 = (bf16[2,96,896]{2,1,0:T(8,128)(2,1)S(1)}, bf16[2,96,896]{2,1,0:T(8,128)(2,1)S(1)}, u32[]{:S(2)}, u32[]{:S(2)}) collective-permute-start(bf16[2,96,896]{2,1,0:T(8,128)(2,1)S(1)} %get-tuple-element.13), channel_id=1, source_target_pairs={{8,0},{16,8},{24,16},{9,1},{17,9},{25,17},{10,2},{18,10},{26,18},{... | collective-permute-start | bytes 1032200 | tf_op jit(solution)/shard_map/ppermute | solution.py:257
  45.1 8.7 %collective-permute-start.12 = (bf16[192,896]{1,0:T(8,128)(2,1)S(1)}, bf16[192,896]{1,0:T(8,128)(2,1)S(1)}, u32[]{:S(2)}, u32[]{:S(2)}) collective-permute-start(bf16[192,896]{1,0:T(8,128)(2,1)S(1)} %bitcast.80), channel_id=1, source_target_pairs={{0,4},{2,6},{4,0},{6,2},{1,5},{3,7},{5,1},{7,3},{8,12},{10,14},{12... | collective-permute-start | bytes 1032200 | tf_op jit(solution)/shard_map/ppermute | solution.py:172
  51.7 11.1 %collective-permute-start.5 = (bf16[192,896]{1,0:T(8,128)(2,1)S(1)}, bf16[192,896]{1,0:T(8,128)(2,1)S(1)}, u32[]{:S(2)}, u32[]{:S(2)}) collective-permute-start(bf16[192,896]{1,0:T(8,128)(2,1)S(1)} %bitcast.85), channel_id=1, source_target_pairs={{0,1},{1,0},{2,3},{3,2},{4,5},{5,4},{6,7},{7,6},{8,9},{9,8},{10,11... | collective-permute-start | bytes 1032200 | tf_op jit(solution)/shard_map/ppermute | solution.py:172
  53.3 13.8 %collective-permute-start.6 = (bf16[192,896]{1,0:T(8,128)(2,1)S(1)}, bf16[192,896]{1,0:T(8,128)(2,1)S(1)}, u32[]{:S(2)}, u32[]{:S(2)}) collective-permute-start(bf16[192,896]{1,0:T(8,128)(2,1)S(1)} %bitcast.81), channel_id=1, source_target_pairs={{0,1},{1,0},{2,3},{3,2},{4,5},{5,4},{6,7},{7,6},{8,9},{9,8},{10,11... | collective-permute-start | bytes 1032200 | tf_op jit(solution)/shard_map/ppermute | solution.py:172
  53.8 13.3 %collective-permute-start.11 = (bf16[192,896]{1,0:T(8,128)(2,1)S(1)}, bf16[192,896]{1,0:T(8,128)(2,1)S(1)}, u32[]{:S(2)}, u32[]{:S(2)}) collective-permute-start(bf16[192,896]{1,0:T(8,128)(2,1)S(1)} %bitcast.86), channel_id=1, source_target_pairs={{0,4},{2,6},{4,0},{6,2},{1,5},{3,7},{5,1},{7,3},{8,12},{10,14},{12... | collective-permute-start | bytes 1032200 | tf_op jit(solution)/shard_map/ppermute | solution.py:172
  62.8 18.0 %collective-permute-start.20 = (bf16[448,896]{1,0:T(8,128)(2,1)}, bf16[448,896]{1,0:T(8,128)(2,1)}, u32[]{:S(2)}, u32[]{:S(2)}) collective-permute-start(bf16[448,896]{1,0:T(8,128)(2,1)} %collective-permute-done.19.refs_17_), channel_id=1, source_target_pairs={{8,16},{16,24},{9,17},{17,25},{10,18},{18,26},{11,19},{19,27},{12,... | collective-permute-start | bytes 2408456 | tf_op jit(solution)/shard_map/ppermute | solution.py:230
  64.4 23.8 %collective-permute-start.23 = (bf16[448,896]{1,0:T(8,128)(2,1)}, bf16[448,896]{1,0:T(8,128)(2,1)}, u32[]{:S(2)}, u32[]{:S(2)}) collective-permute-start(bf16[448,896]{1,0:T(8,128)(2,1)} %collective-permute-done.22.refs_18_), channel_id=1, source_target_pairs={{8,0},{16,8},{9,1},{17,9},{10,2},{18,10},{11,3},{19,11},{12,4},{20... | collective-permute-start | bytes 2408456 | tf_op jit(solution)/shard_map/ppermute | solution.py:231
  67.2 10.6 %collective-permute-start.14 = (bf16[192,896]{1,0:T(8,128)(2,1)S(1)}, bf16[192,896]{1,0:T(8,128)(2,1)}, u32[]{:S(2)}, u32[]{:S(2)}) collective-permute-start(bf16[192,896]{1,0:T(8,128)(2,1)S(1)} %collective-permute-done.12.refs_9_), channel_id=1, source_target_pairs={{0,1},{1,0},{2,3},{3,2},{4,5},{5,4},{6,7},{7,6},{8,9},{9,8},{10,11... | collective-permute-start | bytes 1032200 | tf_op jit(solution)/shard_map/ppermute | solution.py:172
  68.7 10.2 %collective-permute-start.13 = (bf16[192,896]{1,0:T(8,128)(2,1)S(1)}, bf16[192,896]{1,0:T(8,128)(2,1)}, u32[]{:S(2)}, u32[]{:S(2)}) collective-permute-start(bf16[192,896]{1,0:T(8,128)(2,1)S(1)} %collective-permute-done.5.refs_2_), channel_id=1, source_target_pairs={{0,4},{2,6},{4,0},{6,2},{1,5},{3,7},{5,1},{7,3},{8,12},{10,14},{12... | collective-permute-start | bytes 1032200 | tf_op jit(solution)/shard_map/ppermute | solution.py:172
  70.2 8.8 %collective-permute-start.16 = (bf16[192,896]{1,0:T(8,128)(2,1)S(1)}, bf16[192,896]{1,0:T(8,128)(2,1)S(1)}, u32[]{:S(2)}, u32[]{:S(2)}) collective-permute-start(bf16[192,896]{1,0:T(8,128)(2,1)S(1)} %collective-permute-done.12.refs_9_), channel_id=1, source_target_pairs={{0,2},{2,0},{4,6},{6,4},{1,3},{3,1},{5,7},{7,5},{8,10},{10,8},{12,... | collective-permute-start | bytes 1032200 | tf_op jit(solution)/shard_map/ppermute | solution.py:172
  79.0 11.9 %collective-permute-start.15 = (bf16[192,896]{1,0:T(8,128)(2,1)S(1)}, bf16[192,896]{1,0:T(8,128)(2,1)}, u32[]{:S(2)}, u32[]{:S(2)}) collective-permute-start(bf16[192,896]{1,0:T(8,128)(2,1)S(1)} %collective-permute-done.11.refs_8_), channel_id=1, source_target_pairs={{0,2},{2,0},{4,6},{6,4},{1,3},{3,1},{5,7},{7,5},{8,10},{10,8},{12,... | collective-permute-start | bytes 1032200 | tf_op jit(solution)/shard_map/ppermute | solution.py:172
  79.5 11.4 %collective-permute-start.18 = (bf16[192,896]{1,0:T(8,128)(2,1)}, bf16[192,896]{1,0:T(8,128)(2,1)}, u32[]{:S(2)}, u32[]{:S(2)}) collective-permute-start(bf16[192,896]{1,0:T(8,128)(2,1)} %collective-permute-done.14.refs_11_), channel_id=1, source_target_pairs={{0,2},{2,0},{4,6},{6,4},{1,3},{3,1},{5,7},{7,5},{8,10},{10,8},{12,... | collective-permute-start | bytes 1032200 | tf_op jit(solution)/shard_map/ppermute | solution.py:172
  80.6 10.2 %collective-permute-start.17 = (bf16[192,896]{1,0:T(8,128)(2,1)}, bf16[192,896]{1,0:T(8,128)(2,1)}, u32[]{:S(2)}, u32[]{:S(2)}) collective-permute-start(bf16[192,896]{1,0:T(8,128)(2,1)} %collective-permute-done.13.refs_10_), channel_id=1, source_target_pairs={{0,2},{2,0},{4,6},{6,4},{1,3},{3,1},{5,7},{7,5},{8,10},{10,8},{12,... | collective-permute-start | bytes 1032200 | tf_op jit(solution)/shard_map/ppermute | solution.py:172
  80.8 16.8 %collective-permute-start.21 = (bf16[448,896]{1,0:T(8,128)(2,1)}, bf16[448,896]{1,0:T(8,128)(2,1)S(1)}, u32[]{:S(2)}, u32[]{:S(2)}) collective-permute-start(bf16[448,896]{1,0:T(8,128)(2,1)} %collective-permute-done.20.refs_19_), channel_id=1, source_target_pairs={{16,24},{17,25},{18,26},{19,27},{20,28},{21,29},{22,30},{23,31}} | collective-permute-start | bytes 2408456 | tf_op jit(solution)/shard_map/ppermute | solution.py:230
  88.2 21.6 %collective-permute-start.24 = (bf16[448,896]{1,0:T(8,128)(2,1)}, bf16[448,896]{1,0:T(8,128)(2,1)S(1)}, u32[]{:S(2)}, u32[]{:S(2)}) collective-permute-start(bf16[448,896]{1,0:T(8,128)(2,1)} %collective-permute-done.23.refs_20_), channel_id=1, source_target_pairs={{8,0},{9,1},{10,2},{11,3},{12,4},{13,5},{14,6},{15,7}} | collective-permute-start | bytes 2408456 | tf_op jit(solution)/shard_map/ppermute | solution.py:231
  118.3 8.4 %all-to-all-start = ((f32[8,2,2,2,96]{4,3,2,1,0:T(2,128)}), f32[8,2,2,2,96]{4,3,2,1,0:T(2,128)S(1)}, u32[]{:S(2)}, u32[]{:S(2)}) async-start(f32[8,2,2,2,96]{4,3,2,1,0:T(2,128)} %broadcast_in_dim.9), calls=%async_computation | async-start | bytes 65536 | tf_op jit(solution)/shard_map/all_to_all | solution.py:191
  128.2 10.2 %all-to-all-start.1 = ((f32[32,1,450]{2,1,0:T(1,128)}), f32[32,1,450]{2,1,0:T(1,128)S(1)}, u32[]{:S(2)}, u32[]{:S(2)}) async-start(f32[32,1,450]{2,1,0:T(1,128)} %broadcast_in_dim.11), calls=%async_computation.1 | async-start | bytes 131072 | tf_op jit(solution)/shard_map/all_to_all | solution.py:191
  130.8 10.3 %collective-permute-start.25 = (bf16[2,96,448]{2,1,0:T(8,128)(2,1)S(1)}, bf16[2,96,448]{2,1,0:T(8,128)(2,1)S(1)}, u32[]{:S(2)}, u32[]{:S(2)}) collective-permute-start(bf16[2,96,448]{2,1,0:T(8,128)(2,1)S(1)} %select_bitcast_fusion.1), channel_id=1, source_target_pairs={{0,1},{1,0},{2,3},{3,2},{4,5},{5,4},{6,7},{7,6},{8,9},{9,8},{10,11... | collective-permute-start | bytes 516104 | tf_op jit(solution)/shard_map/ppermute | solution.py:172
  (22 other events, 311.9 us)

commit v2 on v1

--- a/solution.py
+++ b/solution.py
@@ -91,7 +91,7 @@
         block_refs = refs[: len(flat)]
         weight_refs = refs[len(flat) : len(flat) + shard_total]
         total_ref = refs[len(flat) + shard_total] if total is not None else None
-        out_ref, rows, held, row_sem, weight_sem = refs[-5:]
+        out_ref, squares_ref, rows, held, row_sem, weight_sem, total_sem = refs[-7:]
 
         def weight_copy(shard):
             return pltpu.make_async_copy(weight_refs[shard], held.at[shard], weight_sem.at[shard])
@@ -121,7 +121,9 @@
                                 row_copy(place, shard, clip, stream).start()
 
         if total is not None:
-            out_ref[...] = total_ref[...]
+            total_copy = pltpu.make_async_copy(total_ref, out_ref, total_sem)
+            total_copy.start()
+            total_copy.wait()
         else:
             out_ref[...] = jnp.zeros_like(out_ref)
 
@@ -141,21 +143,34 @@
                         preferred_element_type=jnp.float32,
                     )
 
+        ones = jnp.ones((8, columns), jnp.float32)
+        for clip in range(clip_count):
+            squares_ref[clip] = lax.dot_general(
+                ones,
+                out_ref[clip] * out_ref[clip],
+                (((1,), (1,)), ((), ())),
+                precision=lax.Precision.HIGHEST,
+                preferred_element_type=jnp.float32,
+            )
+
     operands = [*flat, *weights]
-    in_specs = [pl.BlockSpec(memory_space=pl.ANY) for _ in operands]
     if total is not None:
         operands.append(total)
-        in_specs.append(pl.BlockSpec(memory_space=pltpu.VMEM))
-    return pl.pallas_call(
+    in_specs = [pl.BlockSpec(memory_space=pl.ANY) for _ in operands]
+    total, squares = pl.pallas_call(
         kernel,
         in_specs=[pl.BlockSpec(memory_space=pltpu.SMEM)] + in_specs,
-        out_specs=pl.BlockSpec(memory_space=pltpu.VMEM),
-        out_shape=jax.ShapeDtypeStruct((clip_count, row_count, columns), jnp.float32),
+        out_specs=[pl.BlockSpec(memory_space=pltpu.VMEM)] * 2,
+        out_shape=[
+            jax.ShapeDtypeStruct((clip_count, row_count, columns), jnp.float32),
+            jax.ShapeDtypeStruct((clip_count, 8, row_count), jnp.float32),
+        ],
         scratch_shapes=[
             pltpu.VMEM((shard_total, clip_count * row_count, depth), jnp.bfloat16),
             pltpu.VMEM((shard_total, columns, depth), jnp.bfloat16),
             pltpu.SemaphoreType.DMA((shard_total, clip_count, stream_count)),
             pltpu.SemaphoreType.DMA((shard_total,)),
+            pltpu.SemaphoreType.DMA,
         ],
         compiler_params=pltpu.CompilerParams(vmem_limit_bytes=56 * 1024 * 1024),
         cost_estimate=pl.CostEstimate(
@@ -165,6 +180,7 @@
         ),
         name="project",
     )(scalars, *operands)
+    return total, squares[:, 0]
 
 
 def swap(array, axis, distance):
@@ -221,22 +237,31 @@
     up = [(i, i + 1) for i in range(slab_count - 1)]
     down = [(i + 1, i) for i in range(slab_count - 1)]
 
+    streams = (clean, perturbed)
+    tails = [stream[slots - 1, 1:] for stream in streams]
+    heads = [stream[0, 1:] for stream in streams]
+    tails, heads, out_weight = lax.optimization_barrier((tails, heads, out_weight))
+    left = [lax.ppermute(tail, "frames", up) for tail in tails]
+    right = [lax.ppermute(head, "frames", down) for head in heads]
+
     own_weight = own_columns(out_weight).T
     shards = [(own_weight, slab_index, jnp.int32(1))]
-    line = slab_count == model_count
+    line = slab_count == model_count and slab_count > 2
     if line:
         rising = falling = own_weight
-        for step in range(1, slab_count):
+        last = slab_count - 1
+        across = None
+        for step in range(1, last):
             rising = lax.ppermute(rising, "frames", up[step - 1 :])
             falling = lax.ppermute(falling, "frames", down[: slab_count - step])
             shards += [
                 (rising, jnp.maximum(slab_index - step, 0), slab_index >= step),
-                (
-                    falling,
-                    jnp.minimum(slab_index + step, slab_count - 1),
-                    slab_index < slab_count - step,
-                ),
+                (falling, jnp.minimum(slab_index + step, last), slab_index < slab_count - step),
             ]
+            if across is None:
+                across = lax.ppermute(own_weight, "frames", [(0, last), (last, 0)])
+        at_end = (slab_index == 0) | (slab_index == last)
+        shards.append((across, jnp.where(slab_index == 0, last, 0), at_end))
 
     spread_counts = spread(live_counts[0], distances("dp"))
     counts = [
@@ -249,13 +274,12 @@
     nearby = pick(near_counts, clip_index)
 
     gathered = []
-    for stream, order in (
-        (clean, distances("dp") + distances("mp")),
-        (perturbed, distances("mp")[:1] + distances("dp") + distances("mp")[1:]),
-    ):
-        left = lax.ppermute(stream[slots - 1, 1:], "frames", up)
-        right = lax.ppermute(stream[0, 1:], "frames", down)
-        attended = attention(nearby, stream, left, right)
+    orders = (
+        distances("dp") + distances("mp"),
+        distances("mp")[:1] + distances("dp") + distances("mp")[1:],
+    )
+    for n, order in enumerate(orders):
+        attended = attention(nearby, streams[n], left[n], right[n])
         gathered.append(spread(attended.reshape(near_rows, local_width), order))
     blocks = [
         [[g[m, c] for g in gathered] for c in range(clip_count)] for m in range(model_count)
@@ -272,8 +296,8 @@
         )
 
     if line:
-        total = project_shards(shards[:-2], None)
-        total = project_shards(shards[-2:], total)
+        total, _ = project_shards(shards[:3], None)
+        total, squares = project_shards(shards[3:], total)
     else:
         weight = lax.all_gather(own_weight, "frames", axis=1, tiled=True)
         shards = [
@@ -284,11 +308,12 @@
             )
             for m in range(model_count)
         ]
-        total = project_shards(shards, None)
+        total, squares = project_shards(shards, None)
     projected = total.reshape(clip_count, 2, slots, tile_len, half)
 
-    squares = jnp.sum(collect(jnp.sum(projected * projected, axis=-1), ("mp", "dp")), axis=0)
-    scale = lax.rsqrt(squares / model_width + epsilon)[..., None]
+    squares = jnp.sum(collect(squares, ("mp", "dp")), axis=0)
+    squares = squares.reshape(clip_count, 2, slots, tile_len, 1)
+    scale = lax.rsqrt(squares / model_width + epsilon)
     own_counts = jnp.stack([n[1 : slots + 1] for n in near_counts])
     live = (jnp.arange(tile_len) < own_counts[..., None]).astype(jnp.float32)[..., None]
     gain = own_columns(norm_gain)

time: 144 us -> 156 us (1.083)
  other arithmetic: 5.63 us -> 9.73 us
  waiting for transfers between devices: 62.2 us -> 65.7 us
  local copies, waits for them, and re-layouts: 8.81 us -> 11.1 us
  Pallas kernels: 20.8 us -> 22.9 us
    optimization_barrier x0 -> x1, local copies, waits for them, and re-layouts: none -> 3.58 us  [local(): lax.optimization_barrier((tails, heads, out_weight))]
    ppermute x16, waiting for transfers between devices: 18.7 us -> 22.2 us  [swap(): return lax.ppermute(array, axis, [(i, i ^ distance) for i in range(count)])]
    ppermute x4 -> x5, starting transfers between devices: 11.7 us -> 14.8 us  [the longest x2 9.49 us: local(): left = [lax.ppermute(tail, 'frames', up) for tail in tails]]
    pallas_call x2, Pallas kernels: 11.8 us -> 13.9 us  [project(): pl.pallas_call(kernel, in_specs=[pl.BlockSpec(memory_space=pltpu.SMEM)] +...]
    ppermute x4 -> x5, waiting for transfers between devices: 14.1 us -> 16.1 us  [the longest x1 6.29 us: local(): across = lax.ppermute(own_weight, 'frames', [(0, last), (last, 0)])]
    ppermute x3 -> x2, waiting for transfers between devices: 18.9 us -> 17 us  [local(): falling = lax.ppermute(falling, 'frames', down[:slab_count - step])]
    select_n x5, other arithmetic: 0.23 us -> 2.06 us  [pick(): return lax.select_n(index, *options) if len(options) > 1 else options[0]]
    reduce_sum x2 -> x1, other arithmetic: 1.75 us -> 0.02 us  [local(): squares = jnp.sum(collect(squares, ('mp', 'dp')), axis=0)]
  transfers between devices with their start and end apart: 28 -> 27, of which waited for: 12 -> 11; matrix products, arithmetic and copies ran while one was open for 3% -> 7% of each run, Pallas kernels for 11% -> 10%
where the time goes in v2:
time: 156 us
  waiting for transfers between devices  65.7 us (42%)
  starting transfers between devices  42.6 us (27%)
  Pallas kernels  22.9 us (15%)
  local copies, waits for them, and re-layouts  11.1 us (7%)
  other arithmetic  9.73 us (6%)
  between operations  3.47 us (2%)
    ppermute x16, waiting for transfers between devices, swap(): return lax.ppermute(array, axis, [(i, i ^ distance) for i in range(count)])  22.2 us
    ppermute x2, waiting for transfers between devices, local(): falling = lax.ppermute(falling, 'frames', down[:slab_count - step])  17 us
    pallas_call x2, Pallas kernels, project(): pl.pallas_call(kernel, in_specs=[pl.BlockSpec(memory_space=pltpu.SMEM)] +...  13.9 us
    ppermute x16, starting transfers between devices, swap(): return lax.ppermute(array, axis, [(i, i ^ distance) for i in range(count)])  12.2 us
    all_to_all x2, waiting for transfers between devices, collect(): return lax.all_to_all(copies, axes, split_axis=0, concat_axis=0, tiled=True)  10.5 us
    ppermute x2, starting transfers between devices, local(): left = [lax.ppermute(tail, 'frames', up) for tail in tails]  9.49 us
    pallas_call x2, Pallas kernels, attention(): pl.pallas_call(attend_kernel, grid_spec=pltpu.PrefetchScalarGridSpec(num_...  9 us
    ppermute x2, starting transfers between devices, local(): rising = lax.ppermute(rising, 'frames', up[step - 1:])  6.99 us
  transfers between devices with their start and end apart: 27, of which 11 were waited for; matrix products, arithmetic and copies ran while one was open for 7% of the time, Pallas kernels for 10%

profile of v2, /device:TPU:0, one launch (start us, length us, event | category | flops | bytes accessed | tf_op | source)
XLA Modules:
  0.0 155.6 jit_solution(6119107924967245299)
XLA Ops:
  0.6 1.9 %fusion.own_ref = bf16[2,3,96,896]{3,2,1,0:T(8,128)(2,1)S(1)} fusion(bf16[1,2,96,3,896]{4,2,3,1,0:T(8,128)(2,1)} %param.6, bf16[1,2,96,3,896]{4,2,3,1,0:T(8,128)(2,1)} %param.5), kind=kLoop, calls=%fused_computation.1 | loop fusion | flops 2580480 | bytes 3096576 | tf_op jit(solution)/shard_map/convert_element_type | solution.py:19
  3.7 4.9 %collective-permute-start.3 = (bf16[2,96,896]{2,1,0:T(8,128)(2,1)}, bf16[2,96,896]{2,1,0:T(8,128)(2,1)S(1)}, u32[]{:S(2)}, u32[]{:S(2)}) collective-permute-start(bf16[2,96,896]{2,1,0:T(8,128)(2,1)} %get-tuple-element.13), channel_id=1, source_target_pairs={{0,8},{8,16},{16,24},{1,9},{9,17},{17,25},{2,10},{10,18},{18,26},{... | collective-permute-start | bytes 1032200 | tf_op jit(solution)/shard_map/ppermute | solution.py:244
  9.9 3.6 %copy.20 = bf16[896,896]{0,1:T(8,128)(2,1)} copy(bf16[896,896]{1,0:T(8,128)(2,1)} %param.7) | data formatting | bytes 3211264 | tf_op jit(solution)/shard_map/optimization_barrier | solution.py:243
  15.0 5.4 %collective-permute-start.19 = (bf16[448,896]{1,0:T(8,128)(2,1)S(1)}, bf16[448,896]{1,0:T(8,128)(2,1)}, u32[]{:S(2)}, u32[]{:S(2)}) collective-permute-start(bf16[448,896]{1,0:T(8,128)(2,1)S(1)} %fusion.1.refs_16_), channel_id=1, source_target_pairs={{0,8},{8,16},{16,24},{1,9},{9,17},{17,25},{2,10},{10,18},{18,26},{... | collective-permute-start | bytes 2408456 | tf_op jit(solution)/shard_map/ppermute | solution.py:255
  23.3 2.1 %collective-permute-done = s32[8]{0:T(128)} collective-permute-done((s32[8]{0:T(128)}, s32[8]{0:T(128)}, u32[]{:S(2)}, u32[]{:S(2)}) %collective-permute-start) | collective-permute-done | bytes 64 | tf_op jit(solution)/shard_map/ppermute | solution.py:188
  25.4 4.6 %collective-permute-start.1 = (bf16[2,96,896]{2,1,0:T(8,128)(2,1)}, bf16[2,96,896]{2,1,0:T(8,128)(2,1)S(1)}, u32[]{:S(2)}, u32[]{:S(2)}) collective-permute-start(bf16[2,96,896]{2,1,0:T(8,128)(2,1)} %get-tuple-element.11), channel_id=1, source_target_pairs={{0,8},{8,16},{16,24},{1,9},{9,17},{17,25},{2,10},{10,18},{18,26},{... | collective-permute-start | bytes 1032200 | tf_op jit(solution)/shard_map/ppermute | solution.py:244
  32.7 4.5 %attention.3 = bf16[2,96,896]{2,1,0:T(8,128)(2,1)S(1)} custom-call(s32[4]{0:T(128)S(1)} %get-tuple-element.21.counts_ref, bf16[2,3,96,896]{3,2,1,0:T(8,128)(2,1)S(1)} %fusion.own_ref, bf16[2,96,896]{2,1,0:T(8,128)(2,1)S(1)} %collective-permute-done.3.left_ref, bf16[2,96,896]{2,1,0:T(8,128)(2,1)S(1)} %collective-permute-done.4.right_ref), custom_call_target="tpu_custom_call" | custom-call | flops 4954521600 | bytes 2064384 | tf_op jit(solution)/shard_map/attention/pallas_call | solution.py:62
  38.7 4.9 %collective-permute-done.1.left_ref = bf16[2,96,896]{2,1,0:T(8,128)(2,1)S(1)} collective-permute-done((bf16[2,96,896]{2,1,0:T(8,128)(2,1)}, bf16[2,96,896]{2,1,0:T(8,128)(2,1)S(1)}, u32[]{:S(2)}, u32[]{:S(2)}) %collective-permute-start.1) | collective-permute-done | bytes 344096 | tf_op jit(solution)/shard_map/ppermute | solution.py:244
  43.6 4.9 %collective-permute-done.2.right_ref = bf16[2,96,896]{2,1,0:T(8,128)(2,1)S(1)} collective-permute-done((bf16[2,96,896]{2,1,0:T(8,128)(2,1)}, bf16[2,96,896]{2,1,0:T(8,128)(2,1)S(1)}, u32[]{:S(2)}, u32[]{:S(2)}) %collective-permute-start.2) | collective-permute-done | bytes 344096 | tf_op jit(solution)/shard_map/ppermute | solution.py:245
  48.5 4.5 %attention.2 = bf16[2,96,896]{2,1,0:T(8,128)(2,1)S(1)} custom-call(s32[4]{0:T(128)S(1)} %get-tuple-element.21.counts_ref, bf16[2,3,96,896]{3,2,1,0:T(8,128)(2,1)S(1)} %bitcast.80, bf16[2,96,896]{2,1,0:T(8,128)(2,1)S(1)} %collective-permute-done.1.left_ref, bf16[2,96,896]{2,1,0:T(8,128)(2,1)S(1)} %collective-permute-done.2.right_ref), custom_call_target="tpu_custom_call" | custom-call | flops 4954521600 | bytes 2064384 | tf_op jit(solution)/shard_map/attention/pallas_call | solution.py:62
  53.0 1.6 %collective-permute-start.5 = (bf16[192,896]{1,0:T(8,128)(2,1)S(1)}, bf16[192,896]{1,0:T(8,128)(2,1)S(1)}, u32[]{:S(2)}, u32[]{:S(2)}) collective-permute-start(bf16[192,896]{1,0:T(8,128)(2,1)S(1)} %bitcast.86), channel_id=1, source_target_pairs={{0,1},{1,0},{2,3},{3,2},{4,5},{5,4},{6,7},{7,6},{8,9},{9,8},{10,11... | collective-permute-start | bytes 1032200 | tf_op jit(solution)/shard_map/ppermute | solution.py:188
  56.6 7.5 %collective-permute-done.5.refs_2_ = bf16[192,896]{1,0:T(8,128)(2,1)S(1)} collective-permute-done((bf16[192,896]{1,0:T(8,128)(2,1)S(1)}, bf16[192,896]{1,0:T(8,128)(2,1)S(1)}, u32[]{:S(2)}, u32[]{:S(2)}) %collective-permute-start.5) | collective-permute-done | bytes 344096 | tf_op jit(solution)/shard_map/ppermute | solution.py:188
  64.1 4.4 %collective-permute-done.6.refs_3_ = bf16[192,896]{1,0:T(8,128)(2,1)S(1)} collective-permute-done((bf16[192,896]{1,0:T(8,128)(2,1)S(1)}, bf16[192,896]{1,0:T(8,128)(2,1)S(1)}, u32[]{:S(2)}, u32[]{:S(2)}) %collective-permute-start.6) | collective-permute-done | bytes 344096 | tf_op jit(solution)/shard_map/ppermute | solution.py:188
  72.2 6.8 %collective-permute-done.14.refs_11_ = bf16[192,896]{1,0:T(8,128)(2,1)S(1)} collective-permute-done((bf16[192,896]{1,0:T(8,128)(2,1)S(1)}, bf16[192,896]{1,0:T(8,128)(2,1)S(1)}, u32[]{:S(2)}, u32[]{:S(2)}) %collective-permute-start.14) | collective-permute-done | bytes 344096 | tf_op jit(solution)/shard_map/ppermute | solution.py:188
  80.4 2.7 %collective-permute-start.23 = (bf16[448,896]{1,0:T(8,128)(2,1)S(1)}, bf16[448,896]{1,0:T(8,128)(2,1)}, u32[]{:S(2)}, u32[]{:S(2)}) collective-permute-start(bf16[448,896]{1,0:T(8,128)(2,1)S(1)} %fusion.1.refs_16_), channel_id=1, source_target_pairs={{0,24},{24,0},{1,25},{25,1},{2,26},{26,2},{3,27},{27,3},{4,28},{28... | collective-permute-start | bytes 2408456 | tf_op jit(solution)/shard_map/ppermute | solution.py:262
  90.8 6.3 %project.2 = (f32[2,384,448]{2,1,0:T(8,128)}, f32[2,8,384]{2,1,0:T(8,128)}) custom-call(s32[7]{0:T(128)} %stack.85.scalars_ref, bf16[192,896]{1,0:T(8,128)(2,1)} %bitcast.89, bf16[192,896]{1,0:T(8,128)(2,1)} %bitcast.84, bf16[192,896]{1,0:T(8,128)(2,1)} %copy-done.5, bf16[192,896]{1,0:T(8,128)(2,1)} %copy-done.6, bf16[192,896]{1,0:T(8,128)(2,1)} %copy-done.9, ...), custom_call_target="tpu_custom_call" | custom-call | flops 1849688064 | bytes 6537216 | tf_op jit(solution)/shard_map/project/pallas_call | solution.py:160
  97.2 6.3 %collective-permute-done.23.refs_18_ = bf16[448,896]{1,0:T(8,128)(2,1)} collective-permute-done((bf16[448,896]{1,0:T(8,128)(2,1)S(1)}, bf16[448,896]{1,0:T(8,128)(2,1)}, u32[]{:S(2)}, u32[]{:S(2)}) %collective-permute-start.23) | collective-permute-done | bytes 802848 | tf_op jit(solution)/shard_map/ppermute | solution.py:262
  103.4 17.0 %collective-permute-done.22.refs_17_ = bf16[448,896]{1,0:T(8,128)(2,1)} collective-permute-done((bf16[448,896]{1,0:T(8,128)(2,1)}, bf16[448,896]{1,0:T(8,128)(2,1)}, u32[]{:S(2)}, u32[]{:S(2)}) %collective-permute-start.22) | collective-permute-done | bytes 802848 | tf_op jit(solution)/shard_map/ppermute | solution.py:256
  120.5 7.6 %project.3 = (f32[2,384,448]{2,1,0:T(8,128)}, f32[2,8,384]{2,1,0:T(8,128)}) custom-call(s32[7]{0:T(128)} %stack.77.scalars_ref, bf16[192,896]{1,0:T(8,128)(2,1)} %bitcast.90, bf16[192,896]{1,0:T(8,128)(2,1)} %bitcast.85, bf16[192,896]{1,0:T(8,128)(2,1)} %copy-done.5, bf16[192,896]{1,0:T(8,128)(2,1)} %copy-done.6, bf16[192,896]{1,0:T(8,128)(2,1)} %copy-done.9, ...), custom_call_target="tpu_custom_call" | custom-call | flops 1849688064 | bytes 6537216 | tf_op jit(solution)/shard_map/project/pallas_call | solution.py:160
  129.5 3.6 %all-to-all-start = ((f32[8,2,384]{2,1,0:T(2,128)}), f32[8,2,384]{2,1,0:T(2,128)S(1)}, u32[]{:S(2)}, u32[]{:S(2)}) async-start(f32[8,2,384]{2,1,0:T(2,128)} %broadcast_in_dim.9), calls=%async_computation | async-start | bytes 49152 | tf_op jit(solution)/shard_map/all_to_all | solution.py:207
  133.1 4.6 %all-to-all-done = f32[8,2,384]{2,1,0:T(2,128)S(1)} async-done(((f32[8,2,384]{2,1,0:T(2,128)}), f32[8,2,384]{2,1,0:T(2,128)S(1)}, u32[]{:S(2)}, u32[]{:S(2)}) %all-to-all-start) | async-done | bytes 24608 | tf_op jit(solution)/shard_map/all_to_all | solution.py:207
  140.6 2.6 %all-to-all-start.1 = ((f32[32,1,450]{2,1,0:T(1,128)}), f32[32,1,450]{2,1,0:T(1,128)S(1)}, u32[]{:S(2)}, u32[]{:S(2)}) async-start(f32[32,1,450]{2,1,0:T(1,128)} %broadcast_in_dim.11), calls=%async_computation.1 | async-start | bytes 131072 | tf_op jit(solution)/shard_map/all_to_all | solution.py:207
  143.3 1.7 %collective-permute-start.24 = (bf16[2,96,448]{2,1,0:T(8,128)(2,1)S(1)}, bf16[2,96,448]{2,1,0:T(8,128)(2,1)S(1)}, u32[]{:S(2)}, u32[]{:S(2)}) collective-permute-start(bf16[2,96,448]{2,1,0:T(8,128)(2,1)S(1)} %select_bitcast_fusion), channel_id=1, source_target_pairs={{0,1},{1,0},{2,3},{3,2},{4,5},{5,4},{6,7},{7,6},{8,9},{9,8},{10,11... | collective-permute-start | bytes 516104 | tf_op jit(solution)/shard_map/ppermute | solution.py:188
  145.0 5.9 %all-to-all-done.1 = f32[32,1,450]{2,1,0:T(1,128)S(1)} async-done(((f32[32,1,450]{2,1,0:T(1,128)}), f32[32,1,450]{2,1,0:T(1,128)S(1)}, u32[]{:S(2)}, u32[]{:S(2)}) %all-to-all-start.1) | async-done | bytes 57632 | tf_op jit(solution)/shard_map/all_to_all | solution.py:207
  (105 shorter events, 32.3 us)
Async XLA Ops:
  3.7 27.7 %collective-permute-start.3 = (bf16[2,96,896]{2,1,0:T(8,128)(2,1)}, bf16[2,96,896]{2,1,0:T(8,128)(2,1)S(1)}, u32[]{:S(2)}, u32[]{:S(2)}) collective-permute-start(bf16[2,96,896]{2,1,0:T(8,128)(2,1)} %get-tuple-element.13), channel_id=1, source_target_pairs={{0,8},{8,16},{16,24},{1,9},{9,17},{17,25},{2,10},{10,18},{18,26},{... | collective-permute-start | bytes 1032200 | tf_op jit(solution)/shard_map/ppermute | solution.py:244
  8.6 24.0 %collective-permute-start.4 = (bf16[2,96,896]{2,1,0:T(8,128)(2,1)}, bf16[2,96,896]{2,1,0:T(8,128)(2,1)S(1)}, u32[]{:S(2)}, u32[]{:S(2)}) collective-permute-start(bf16[2,96,896]{2,1,0:T(8,128)(2,1)} %get-tuple-element.14), channel_id=1, source_target_pairs={{8,0},{16,8},{24,16},{9,1},{17,9},{25,17},{10,2},{18,10},{26,18},{... | collective-permute-start | bytes 1032200 | tf_op jit(solution)/shard_map/ppermute | solution.py:245
  15.0 56.6 %collective-permute-start.19 = (bf16[448,896]{1,0:T(8,128)(2,1)S(1)}, bf16[448,896]{1,0:T(8,128)(2,1)}, u32[]{:S(2)}, u32[]{:S(2)}) collective-permute-start(bf16[448,896]{1,0:T(8,128)(2,1)S(1)} %fusion.1.refs_16_), channel_id=1, source_target_pairs={{0,8},{8,16},{16,24},{1,9},{9,17},{17,25},{2,10},{10,18},{18,26},{... | collective-permute-start | bytes 2408456 | tf_op jit(solution)/shard_map/ppermute | solution.py:255
  20.5 51.7 %collective-permute-start.21 = (bf16[448,896]{1,0:T(8,128)(2,1)S(1)}, bf16[448,896]{1,0:T(8,128)(2,1)}, u32[]{:S(2)}, u32[]{:S(2)}) collective-permute-start(bf16[448,896]{1,0:T(8,128)(2,1)S(1)} %fusion.1.refs_16_), channel_id=1, source_target_pairs={{8,0},{16,8},{24,16},{9,1},{17,9},{25,17},{10,2},{18,10},{26,18},{... | collective-permute-start | bytes 2408456 | tf_op jit(solution)/shard_map/ppermute | solution.py:256
  25.4 18.2 %collective-permute-start.1 = (bf16[2,96,896]{2,1,0:T(8,128)(2,1)}, bf16[2,96,896]{2,1,0:T(8,128)(2,1)S(1)}, u32[]{:S(2)}, u32[]{:S(2)}) collective-permute-start(bf16[2,96,896]{2,1,0:T(8,128)(2,1)} %get-tuple-element.11), channel_id=1, source_target_pairs={{0,8},{8,16},{16,24},{1,9},{9,17},{17,25},{2,10},{10,18},{18,26},{... | collective-permute-start | bytes 1032200 | tf_op jit(solution)/shard_map/ppermute | solution.py:244
  31.4 17.2 %collective-permute-start.2 = (bf16[2,96,896]{2,1,0:T(8,128)(2,1)}, bf16[2,96,896]{2,1,0:T(8,128)(2,1)S(1)}, u32[]{:S(2)}, u32[]{:S(2)}) collective-permute-start(bf16[2,96,896]{2,1,0:T(8,128)(2,1)} %get-tuple-element.12), channel_id=1, source_target_pairs={{8,0},{16,8},{24,16},{9,1},{17,9},{25,17},{10,2},{18,10},{26,18},{... | collective-permute-start | bytes 1032200 | tf_op jit(solution)/shard_map/ppermute | solution.py:245
  37.2 17.9 %collective-permute-start.12 = (bf16[192,896]{1,0:T(8,128)(2,1)S(1)}, bf16[192,896]{1,0:T(8,128)(2,1)S(1)}, u32[]{:S(2)}, u32[]{:S(2)}) collective-permute-start(bf16[192,896]{1,0:T(8,128)(2,1)S(1)} %bitcast.81), channel_id=1, source_target_pairs={{0,4},{2,6},{4,0},{6,2},{1,5},{3,7},{5,1},{7,3},{8,12},{10,14},{12... | collective-permute-start | bytes 1032200 | tf_op jit(solution)/shard_map/ppermute | solution.py:188
  53.0 11.1 %collective-permute-start.5 = (bf16[192,896]{1,0:T(8,128)(2,1)S(1)}, bf16[192,896]{1,0:T(8,128)(2,1)S(1)}, u32[]{:S(2)}, u32[]{:S(2)}) collective-permute-start(bf16[192,896]{1,0:T(8,128)(2,1)S(1)} %bitcast.86), channel_id=1, source_target_pairs={{0,1},{1,0},{2,3},{3,2},{4,5},{5,4},{6,7},{7,6},{8,9},{9,8},{10,11... | collective-permute-start | bytes 1032200 | tf_op jit(solution)/shard_map/ppermute | solution.py:188
  54.6 13.9 %collective-permute-start.6 = (bf16[192,896]{1,0:T(8,128)(2,1)S(1)}, bf16[192,896]{1,0:T(8,128)(2,1)S(1)}, u32[]{:S(2)}, u32[]{:S(2)}) collective-permute-start(bf16[192,896]{1,0:T(8,128)(2,1)S(1)} %bitcast.82), channel_id=1, source_target_pairs={{0,1},{1,0},{2,3},{3,2},{4,5},{5,4},{6,7},{7,6},{8,9},{9,8},{10,11... | collective-permute-start | bytes 1032200 | tf_op jit(solution)/shard_map/ppermute | solution.py:188
  55.1 13.4 %collective-permute-start.11 = (bf16[192,896]{1,0:T(8,128)(2,1)S(1)}, bf16[192,896]{1,0:T(8,128)(2,1)S(1)}, u32[]{:S(2)}, u32[]{:S(2)}) collective-permute-start(bf16[192,896]{1,0:T(8,128)(2,1)S(1)} %bitcast.87), channel_id=1, source_target_pairs={{0,4},{2,6},{4,0},{6,2},{1,5},{3,7},{5,1},{7,3},{8,12},{10,14},{12... | collective-permute-start | bytes 1032200 | tf_op jit(solution)/shard_map/ppermute | solution.py:188
  64.1 6.0 %collective-permute-start.8 = (bf16[192,896]{1,0:T(8,128)(2,1)S(1)}, bf16[192,896]{1,0:T(8,128)(2,1)S(1)}, u32[]{:S(2)}, u32[]{:S(2)}) collective-permute-start(bf16[192,896]{1,0:T(8,128)(2,1)S(1)} %bitcast.83), channel_id=1, source_target_pairs={{0,2},{2,0},{4,6},{6,4},{1,3},{3,1},{5,7},{7,5},{8,10},{10,8},{12,... | collective-permute-start | bytes 1032200 | tf_op jit(solution)/shard_map/ppermute | solution.py:188
  68.5 10.5 %collective-permute-start.14 = (bf16[192,896]{1,0:T(8,128)(2,1)S(1)}, bf16[192,896]{1,0:T(8,128)(2,1)S(1)}, u32[]{:S(2)}, u32[]{:S(2)}) collective-permute-start(bf16[192,896]{1,0:T(8,128)(2,1)S(1)} %collective-permute-done.12.refs_9_), channel_id=1, source_target_pairs={{0,1},{1,0},{2,3},{3,2},{4,5},{5,4},{6,7},{7,6},{8,9},{9,8},{10,11... | collective-permute-start | bytes 1032200 | tf_op jit(solution)/shard_map/ppermute | solution.py:188
  70.1 10.2 %collective-permute-start.13 = (bf16[192,896]{1,0:T(8,128)(2,1)S(1)}, bf16[192,896]{1,0:T(8,128)(2,1)}, u32[]{:S(2)}, u32[]{:S(2)}) collective-permute-start(bf16[192,896]{1,0:T(8,128)(2,1)S(1)} %collective-permute-done.5.refs_2_), channel_id=1, source_target_pairs={{0,4},{2,6},{4,0},{6,2},{1,5},{3,7},{5,1},{7,3},{8,12},{10,14},{12... | collective-permute-start | bytes 1032200 | tf_op jit(solution)/shard_map/ppermute | solution.py:188
  71.6 11.5 %collective-permute-start.16 = (bf16[192,896]{1,0:T(8,128)(2,1)S(1)}, bf16[192,896]{1,0:T(8,128)(2,1)S(1)}, u32[]{:S(2)}, u32[]{:S(2)}) collective-permute-start(bf16[192,896]{1,0:T(8,128)(2,1)S(1)} %collective-permute-done.12.refs_9_), channel_id=1, source_target_pairs={{0,2},{2,0},{4,6},{6,4},{1,3},{3,1},{5,7},{7,5},{8,10},{10,8},{12,... | collective-permute-start | bytes 1032200 | tf_op jit(solution)/shard_map/ppermute | solution.py:188
  71.6 13.0 %collective-permute-start.9 = (bf16[192,896]{1,0:T(8,128)(2,1)S(1)}, bf16[192,896]{1,0:T(8,128)(2,1)S(1)}, u32[]{:S(2)}, u32[]{:S(2)}) collective-permute-start(bf16[192,896]{1,0:T(8,128)(2,1)S(1)} %collective-permute-done.5.refs_2_), channel_id=1, source_target_pairs={{0,2},{2,0},{4,6},{6,4},{1,3},{3,1},{5,7},{7,5},{8,10},{10,8},{12,... | collective-permute-start | bytes 1032200 | tf_op jit(solution)/shard_map/ppermute | solution.py:188
  72.1 13.8 %collective-permute-start.10 = (bf16[192,896]{1,0:T(8,128)(2,1)S(1)}, bf16[192,896]{1,0:T(8,128)(2,1)S(1)}, u32[]{:S(2)}, u32[]{:S(2)}) collective-permute-start(bf16[192,896]{1,0:T(8,128)(2,1)S(1)} %collective-permute-done.6.refs_3_), channel_id=1, source_target_pairs={{0,2},{2,0},{4,6},{6,4},{1,3},{3,1},{5,7},{7,5},{8,10},{10,8},{12,... | collective-permute-start | bytes 1032200 | tf_op jit(solution)/shard_map/ppermute | solution.py:188
  79.0 7.0 %collective-permute-start.15 = (bf16[192,896]{1,0:T(8,128)(2,1)S(1)}, bf16[192,896]{1,0:T(8,128)(2,1)S(1)}, u32[]{:S(2)}, u32[]{:S(2)}) collective-permute-start(bf16[192,896]{1,0:T(8,128)(2,1)S(1)} %collective-permute-done.11.refs_8_), channel_id=1, source_target_pairs={{0,2},{2,0},{4,6},{6,4},{1,3},{3,1},{5,7},{7,5},{8,10},{10,8},{12,... | collective-permute-start | bytes 1032200 | tf_op jit(solution)/shard_map/ppermute | solution.py:188
  80.4 23.1 %collective-permute-start.23 = (bf16[448,896]{1,0:T(8,128)(2,1)S(1)}, bf16[448,896]{1,0:T(8,128)(2,1)}, u32[]{:S(2)}, u32[]{:S(2)}) collective-permute-start(bf16[448,896]{1,0:T(8,128)(2,1)S(1)} %fusion.1.refs_16_), channel_id=1, source_target_pairs={{0,24},{24,0},{1,25},{25,1},{2,26},{26,2},{3,27},{27,3},{4,28},{28... | collective-permute-start | bytes 2408456 | tf_op jit(solution)/shard_map/ppermute | solution.py:262
  83.1 20.4 %collective-permute-start.20 = (bf16[448,896]{1,0:T(8,128)(2,1)}, bf16[448,896]{1,0:T(8,128)(2,1)}, u32[]{:S(2)}, u32[]{:S(2)}) collective-permute-start(bf16[448,896]{1,0:T(8,128)(2,1)} %collective-permute-done.19.refs_17_), channel_id=1, source_target_pairs={{8,16},{16,24},{9,17},{17,25},{10,18},{18,26},{11,19},{19,27},{12,... | collective-permute-start | bytes 2408456 | tf_op jit(solution)/shard_map/ppermute | solution.py:255
  84.6 35.9 %collective-permute-start.22 = (bf16[448,896]{1,0:T(8,128)(2,1)}, bf16[448,896]{1,0:T(8,128)(2,1)}, u32[]{:S(2)}, u32[]{:S(2)}) collective-permute-start(bf16[448,896]{1,0:T(8,128)(2,1)} %collective-permute-done.21.refs_18_), channel_id=1, source_target_pairs={{8,0},{16,8},{9,1},{17,9},{10,2},{18,10},{11,3},{19,11},{12,4},{20... | collective-permute-start | bytes 2408456 | tf_op jit(solution)/shard_map/ppermute | solution.py:256
  85.9 4.8 %collective-permute-start.18 = (bf16[192,896]{1,0:T(8,128)(2,1)S(1)}, bf16[192,896]{1,0:T(8,128)(2,1)}, u32[]{:S(2)}, u32[]{:S(2)}) collective-permute-start(bf16[192,896]{1,0:T(8,128)(2,1)S(1)} %collective-permute-done.14.refs_11_), channel_id=1, source_target_pairs={{0,2},{2,0},{4,6},{6,4},{1,3},{3,1},{5,7},{7,5},{8,10},{10,8},{12,... | collective-permute-start | bytes 1032200 | tf_op jit(solution)/shard_map/ppermute | solution.py:188
  129.5 8.3 %all-to-all-start = ((f32[8,2,384]{2,1,0:T(2,128)}), f32[8,2,384]{2,1,0:T(2,128)S(1)}, u32[]{:S(2)}, u32[]{:S(2)}) async-start(f32[8,2,384]{2,1,0:T(2,128)} %broadcast_in_dim.9), calls=%async_computation | async-start | bytes 49152 | tf_op jit(solution)/shard_map/all_to_all | solution.py:207
  140.6 10.2 %all-to-all-start.1 = ((f32[32,1,450]{2,1,0:T(1,128)}), f32[32,1,450]{2,1,0:T(1,128)S(1)}, u32[]{:S(2)}, u32[]{:S(2)}) async-start(f32[32,1,450]{2,1,0:T(1,128)} %broadcast_in_dim.11), calls=%async_computation.1 | async-start | bytes 131072 | tf_op jit(solution)/shard_map/all_to_all | solution.py:207
  143.3 10.3 %collective-permute-start.24 = (bf16[2,96,448]{2,1,0:T(8,128)(2,1)S(1)}, bf16[2,96,448]{2,1,0:T(8,128)(2,1)S(1)}, u32[]{:S(2)}, u32[]{:S(2)}) collective-permute-start(bf16[2,96,448]{2,1,0:T(8,128)(2,1)S(1)} %select_bitcast_fusion), channel_id=1, source_target_pairs={{0,1},{1,0},{2,3},{3,2},{4,5},{5,4},{6,7},{7,6},{8,9},{9,8},{10,11... | collective-permute-start | bytes 516104 | tf_op jit(solution)/shard_map/ppermute | solution.py:188
  (22 other events, 389.3 us)
